TPU v7x, 512 devices: a whole 4x8x8 slice. The times are simulated.
512 devices in a mesh: grp: 16 (over y_lo, z), blk: 32 (over x, y_hi, core).
Axes of the slice: x: 4, y: 8 (y_hi: 4, y_lo: 2; y = y_hi * 2 + y_lo), z: 8, core: 2. Of those that a mesh axis runs over, the one named last changes fastest.
Arguments:
- image_embed: bfloat16 [262144, 1152], P(('grp', 'blk')), may hold values from -2 to 2
- text_embed: bfloat16 [262144, 1152], P(('grp', 'blk')), may hold values from -2 to 2
- log_scale: float32 [1], replicated, may hold values from 1.5 to 2.5
- bias: float32 [1], replicated, may hold values from -4 to -2
Outputs:
- image_grad: bfloat16 [262144, 1152], P(('grp', 'blk'))
- text_grad: bfloat16 [262144, 1152], P(('grp', 'blk'))
- row_loss: float32 [262144], P(('grp', 'blk'))
All inputs are finite; a program needn't handle non-finite values.
Results may differ from a plain program's by a relative error of at most 0.0063.
Values may be sent and summed in bfloat16 or wider, within the bound.
No kernel may reach another device: no remote copies, remote signals or barrier semaphores. Data moves between devices by JAX's collectives and lax.ppermute only.
A program may use at most 64 MiB of HBM per device.

v0:
```python
import jax
import jax.numpy as jnp
from jax import lax
from jax.sharding import PartitionSpec as P


def shifted(array, axis, by):
    size = lax.axis_size(axis)
    return lax.ppermute(array, axis, [(i, (i + by) % size) for i in range(size)])


def unit_rows(values):
    widened = values.astype(jnp.float32)
    inverse = lax.rsqrt(jnp.sum(widened * widened, axis=1, keepdims=True) + 1e-06)
    return (widened * inverse, inverse)


def logit_weights(scores, logit_scale, logit_bias, positive):
    logits = logit_scale * scores + logit_bias
    weights = (logit_scale * (jax.nn.sigmoid(logits) - positive)).astype(jnp.bfloat16)
    return (weights, logits)


def tangent(units, inverse, summed):
    inner = jnp.sum(units * summed, axis=1, keepdims=True)
    return (inverse * (summed - units * inner)).astype(jnp.bfloat16)


def on_device(image_embed, text_embed, log_scale, bias):
    block_rows = image_embed.shape[0]
    image_units, image_inverse = unit_rows(image_embed)
    text_units, text_inverse = unit_rows(text_embed)
    image_low = image_units.astype(jnp.bfloat16)
    text_low = text_units.astype(jnp.bfloat16)
    logit_scale = jnp.exp(log_scale[0])
    logit_bias = bias[0]
    left_text = shifted(text_low, "blk", 1)
    right_text = shifted(text_low, "blk", -1)
    upper_text = shifted(text_low, "grp", 1)
    visiting = jnp.concatenate([text_low, left_text, right_text, upper_text], axis=0)
    scores = lax.dot_general(
        image_low, visiting, (((1,), (1,)), ((), ())), preferred_element_type=jnp.float32
    )
    positive = (
        jnp.arange(block_rows, dtype=jnp.int32)[:, None]
        == jnp.arange(4 * block_rows, dtype=jnp.int32)[None, :]
    ).astype(jnp.float32)
    weights, logits = logit_weights(scores, logit_scale, logit_bias, positive)
    row_loss = jnp.mean(jax.nn.softplus(jnp.where(positive > 0, -logits, logits)), axis=1)
    image_sum = jnp.dot(weights, visiting, preferred_element_type=jnp.float32)
    contrib = lax.dot_general(
        weights, image_low, (((0,), (0,)), ((), ())), preferred_element_type=jnp.float32
    )
    own_part = contrib[:block_rows]
    to_left = contrib[block_rows : 2 * block_rows].astype(jnp.bfloat16)
    to_right = contrib[2 * block_rows : 3 * block_rows].astype(jnp.bfloat16)
    to_upper = contrib[3 * block_rows :].astype(jnp.bfloat16)
    from_next = shifted(to_left, "blk", -1)
    from_prev = shifted(to_right, "blk", 1)
    from_below = shifted(to_upper, "grp", -1)
    text_sum = (
        own_part
        + from_next.astype(jnp.float32)
        + from_prev.astype(jnp.float32)
        + from_below.astype(jnp.float32)
    )
    image_grad = tangent(image_units, image_inverse, image_sum)
    text_grad = tangent(text_units, text_inverse, text_sum)
    return (image_grad, text_grad, row_loss)


def solution(mesh):
    placed = (P(("grp", "blk"), None), P(("grp", "blk"), None), P(), P())
    return jax.shard_map(
        on_device,
        mesh=mesh,
        in_specs=placed,
        out_specs=(P(("grp", "blk"), None), P(("grp", "blk"), None), P(("grp", "blk"))),
        check_vma=False,
    )
```

profile of v0, /device:TPU:1, one launch (start us, length us, event | category | flops | bytes accessed | tf_op | source)
XLA Modules:
  0.0 134.7 jit_solution(18281780653486747674)
XLA Ops:
  0.6 1.6 %copy.7 = bf16[512,1152]{0,1:T(8,128)(2,1)S(1)} copy(bf16[512,1152]{1,0:T(8,128)(2,1)} %param.5) | data formatting | bytes 2359296 | tf_op args[1]
  2.2 0.0 copy-start
  2.2 0.3 fusion.20
  2.5 0.2 fusion.7
  2.8 4.8 %collective-permute-start.2 = (bf16[512,1152]{0,1:T(8,128)(2,1)S(1)}, bf16[512,1152]{0,1:T(8,128)(2,1)S(1)}, u32[]{:S(2)}, u32[]{:S(2)}) collective-permute-start(bf16[512,1152]{0,1:T(8,128)(2,1)S(1)} %fusion.7), channel_id=1, source_target_pairs={{0,32},{32,64},{64,96},{96,128},{128,160},{160,192},{192,224},{224... | collective-permute-start | bytes 3538952 | tf_op jit(solution)/shard_map/ppermute | solution.py:9
  7.6 5.9 %collective-permute-start.1 = (bf16[512,1152]{0,1:T(8,128)(2,1)S(1)}, bf16[512,1152]{0,1:T(8,128)(2,1)S(1)}, u32[]{:S(2)}, u32[]{:S(2)}) collective-permute-start(bf16[512,1152]{0,1:T(8,128)(2,1)S(1)} %fusion.7), channel_id=1, source_target_pairs={{0,31},{1,0},{2,1},{3,2},{4,3},{5,4},{6,5},{7,6},{8,7},{9,8},{10,9... | collective-permute-start | bytes 3538952 | tf_op jit(solution)/shard_map/ppermute | solution.py:9
  13.5 1.9 %collective-permute-start = (bf16[512,1152]{0,1:T(8,128)(2,1)S(1)}, bf16[512,1152]{0,1:T(8,128)(2,1)S(1)}, u32[]{:S(2)}, u32[]{:S(2)}) collective-permute-start(bf16[512,1152]{0,1:T(8,128)(2,1)S(1)} %fusion.7), channel_id=1, source_target_pairs={{0,1},{1,2},{2,3},{3,4},{4,5},{5,6},{6,7},{7,8},{8,9},{9,10},{10,1... | collective-permute-start | bytes 3538952 | tf_op jit(solution)/shard_map/ppermute | solution.py:9
  16.8 0.0 copy-done
  16.8 0.3 fusion.15
  17.1 36.5 %collective-permute-done.2 = bf16[512,1152]{0,1:T(8,128)(2,1)S(1)} collective-permute-done((bf16[512,1152]{0,1:T(8,128)(2,1)S(1)}, bf16[512,1152]{0,1:T(8,128)(2,1)S(1)}, u32[]{:S(2)}, u32[]{:S(2)}) %collective-permute-start.2) | collective-permute-done | bytes 1179680 | tf_op jit(solution)/shard_map/ppermute | solution.py:9
  53.6 0.0 collective-permute-done.1
  53.6 0.0 collective-permute-done
  53.6 0.0 copy-start.1
  53.6 4.3 %fusion.4 = (f32[512]{0:T(512)S(1)}, f32[512,2048]{1,0:T(8,128)S(1)}) fusion(f32[]{:T(128)} %bitcast.3, f32[]{:T(128)} %bitcast, bf16[512,1152]{0,1:T(8,128)(2,1)S(1)} %collective-permute-done.2, bf16[512,1152]{0,1:T(8,128)(2,1)S(1)} %collective-permute-done.1, bf16[512,1152]{0,1:T(8,128)(2,1)S(1)} %collective-permute-done, ...), kind=kOutput, calls=%fused_computation.10 | convolution fusion | flops 2451242496 | bytes 10096648 | tf_op jit(solution)/shard_map/dot_general | solution.py:41
  57.9 0.0 copy-done.1
  57.9 0.0 copy-start.2
  57.9 2.9 %fusion.33 = (bf16[2048,1152]{0,1:T(8,128)(2,1)S(1)}, f32[2048,1152]{0,1:T(8,128)S(1)}) fusion(bf16[512,1152]{1,0:T(8,128)(2,1)S(1)} %copy-done, f32[512]{0:T(512)S(1)} %add_rsqrt_fusion.1, f32[512,2048]{1,0:T(8,128)S(1)} %get-tuple-element.14, f32[]{:T(128)} %bitcast.4, f32[]{:T(128)} %bitcast), kind=kOutput, calls=%fused_computation.45 | convolution fusion | flops 2430533632 | bytes 19531784 | tf_op jit(solution)/shard_map/dot_general | solution.py:51
  60.8 0.0 copy-done.2
  60.8 0.3 fusion.32
  61.1 3.1 %collective-permute-start.3 = (bf16[512,1152]{0,1:T(8,128)(2,1)S(1)}, bf16[512,1152]{0,1:T(8,128)(2,1)S(1)}, u32[]{:S(2)}, u32[]{:S(2)}) collective-permute-start(bf16[512,1152]{0,1:T(8,128)(2,1)S(1)} %get-tuple-element.6), channel_id=1, source_target_pairs={{0,31},{1,0},{2,1},{3,2},{4,3},{5,4},{6,5},{7,6},{8,7},{9,8},{10,9... | collective-permute-start | bytes 3538952 | tf_op jit(solution)/shard_map/ppermute | solution.py:9
  64.3 16.2 %collective-permute-start.5 = (bf16[512,1152]{0,1:T(8,128)(2,1)S(1)}, bf16[512,1152]{0,1:T(8,128)(2,1)S(1)}, u32[]{:S(2)}, u32[]{:S(2)}) collective-permute-start(bf16[512,1152]{0,1:T(8,128)(2,1)S(1)} %get-tuple-element.7), channel_id=1, source_target_pairs={{0,480},{32,0},{64,32},{96,64},{128,96},{160,128},{192,160},{224,1... | collective-permute-start | bytes 3538952 | tf_op jit(solution)/shard_map/ppermute | solution.py:9
  80.4 5.0 %collective-permute-start.4 = (bf16[512,1152]{0,1:T(8,128)(2,1)S(1)}, bf16[512,1152]{0,1:T(8,128)(2,1)S(1)}, u32[]{:S(2)}, u32[]{:S(2)}) collective-permute-start(bf16[512,1152]{0,1:T(8,128)(2,1)S(1)} %get-tuple-element.8), channel_id=1, source_target_pairs={{0,1},{1,2},{2,3},{3,4},{4,5},{5,6},{6,7},{7,8},{8,9},{9,10},{10,1... | collective-permute-start | bytes 3538952 | tf_op jit(solution)/shard_map/ppermute | solution.py:9
  85.5 6.1 %fusion.11 = (f32[512]{0:T(512)S(1)}, f32[512,1152]{1,0:T(8,128)S(1)}) fusion(bf16[512,1152]{1,0:T(8,128)(2,1)S(1)} %copy-done, f32[512]{0:T(512)S(1)} %add_rsqrt_fusion.1, bf16[512,1152]{0,1:T(8,128)(2,1)S(1)} %collective-permute-done.2, bf16[512,1152]{0,1:T(8,128)(2,1)S(1)} %collective-permute-done.1, bf16[512,1152]{0,1:T(8,128)(2,1)} %copy-done.1, ...), kind=kOutput, calls=%fused_computation.23 | convolution fusion | flops 2447638016 | bytes 12455944 | tf_op jit(solution)/shard_map/dot_general | solution.py:50
  91.6 0.6 broadcast_multiply_fusion
  92.2 1.5 %fusion.14 = bf16[512,1152]{1,0:T(8,128)(2,1)} fusion(f32[512,1152]{1,0:T(8,128)S(1)} %get-tuple-element.10, bf16[512,1152]{1,0:T(8,128)(2,1)S(1)} %copy-done, f32[512]{0:T(512)S(1)} %get-tuple-element.9, f32[512]{0:T(512)S(1)} %add_rsqrt_fusion.1), kind=kLoop, calls=%fused_computation.26 | loop fusion | flops 3538944 | bytes 4722688 | tf_op jit(solution)/shard_map/convert_element_type | solution.py:26
  93.7 0.0 collective-permute-done.3
  93.7 20.9 %collective-permute-done.5 = bf16[512,1152]{0,1:T(8,128)(2,1)S(1)} collective-permute-done((bf16[512,1152]{0,1:T(8,128)(2,1)S(1)}, bf16[512,1152]{0,1:T(8,128)(2,1)S(1)}, u32[]{:S(2)}, u32[]{:S(2)}) %collective-permute-start.5) | collective-permute-done | bytes 1179680 | tf_op jit(solution)/shard_map/ppermute | solution.py:9
  114.6 16.9 %collective-permute-done.4 = bf16[512,1152]{0,1:T(8,128)(2,1)S(1)} collective-permute-done((bf16[512,1152]{0,1:T(8,128)(2,1)S(1)}, bf16[512,1152]{0,1:T(8,128)(2,1)S(1)}, u32[]{:S(2)}, u32[]{:S(2)}) %collective-permute-start.4) | collective-permute-done | bytes 1179680 | tf_op jit(solution)/shard_map/ppermute | solution.py:9
  131.5 0.8 fusion.16
  132.3 0.9 fusion.19
  133.3 1.4 %copy.8 = bf16[512,1152]{1,0:T(8,128)(2,1)} copy(bf16[512,1152]{0,1:T(8,128)(2,1)S(1)} %fusion.19) | data formatting | bytes 2359296
  (2 shorter events, 0.0 us)
Async XLA Ops:
  2.2 14.6 %copy-start = (bf16[512,1152]{1,0:T(8,128)(2,1)S(1)}, bf16[512,1152]{1,0:T(8,128)(2,1)}, u32[]{:S(2)}) copy-start(bf16[512,1152]{1,0:T(8,128)(2,1)} %param.4) | copy-start | bytes 3538948
  2.8 50.8 %collective-permute-start.2 = (bf16[512,1152]{0,1:T(8,128)(2,1)S(1)}, bf16[512,1152]{0,1:T(8,128)(2,1)S(1)}, u32[]{:S(2)}, u32[]{:S(2)}) collective-permute-start(bf16[512,1152]{0,1:T(8,128)(2,1)S(1)} %fusion.7), channel_id=1, source_target_pairs={{0,32},{32,64},{64,96},{96,128},{128,160},{160,192},{192,224},{224... | collective-permute-start | bytes 3538952 | tf_op jit(solution)/shard_map/ppermute | solution.py:9
  7.6 46.0 %collective-permute-start.1 = (bf16[512,1152]{0,1:T(8,128)(2,1)S(1)}, bf16[512,1152]{0,1:T(8,128)(2,1)S(1)}, u32[]{:S(2)}, u32[]{:S(2)}) collective-permute-start(bf16[512,1152]{0,1:T(8,128)(2,1)S(1)} %fusion.7), channel_id=1, source_target_pairs={{0,31},{1,0},{2,1},{3,2},{4,3},{5,4},{6,5},{7,6},{8,7},{9,8},{10,9... | collective-permute-start | bytes 3538952 | tf_op jit(solution)/shard_map/ppermute | solution.py:9
  13.5 40.1 %collective-permute-start = (bf16[512,1152]{0,1:T(8,128)(2,1)S(1)}, bf16[512,1152]{0,1:T(8,128)(2,1)S(1)}, u32[]{:S(2)}, u32[]{:S(2)}) collective-permute-start(bf16[512,1152]{0,1:T(8,128)(2,1)S(1)} %fusion.7), channel_id=1, source_target_pairs={{0,1},{1,2},{2,3},{3,4},{4,5},{5,6},{6,7},{7,8},{8,9},{9,10},{10,1... | collective-permute-start | bytes 3538952 | tf_op jit(solution)/shard_map/ppermute | solution.py:9
  53.6 4.3 %copy-start.1 = (bf16[512,1152]{0,1:T(8,128)(2,1)}, bf16[512,1152]{0,1:T(8,128)(2,1)S(1)}, u32[]{:S(2)}) copy-start(bf16[512,1152]{0,1:T(8,128)(2,1)S(1)} %collective-permute-done) | copy-start | bytes 3538948
  57.9 2.9 %copy-start.2 = (f32[512,2048]{1,0:T(8,128)}, f32[512,2048]{1,0:T(8,128)S(1)}, u32[]{:S(2)}) copy-start(f32[512,2048]{1,0:T(8,128)S(1)} %get-tuple-element.14) | copy-start | bytes 12582916
  61.1 32.6 %collective-permute-start.3 = (bf16[512,1152]{0,1:T(8,128)(2,1)S(1)}, bf16[512,1152]{0,1:T(8,128)(2,1)S(1)}, u32[]{:S(2)}, u32[]{:S(2)}) collective-permute-start(bf16[512,1152]{0,1:T(8,128)(2,1)S(1)} %get-tuple-element.6), channel_id=1, source_target_pairs={{0,31},{1,0},{2,1},{3,2},{4,3},{5,4},{6,5},{7,6},{8,7},{9,8},{10,9... | collective-permute-start | bytes 3538952 | tf_op jit(solution)/shard_map/ppermute | solution.py:9
  64.3 50.3 %collective-permute-start.5 = (bf16[512,1152]{0,1:T(8,128)(2,1)S(1)}, bf16[512,1152]{0,1:T(8,128)(2,1)S(1)}, u32[]{:S(2)}, u32[]{:S(2)}) collective-permute-start(bf16[512,1152]{0,1:T(8,128)(2,1)S(1)} %get-tuple-element.7), channel_id=1, source_target_pairs={{0,480},{32,0},{64,32},{96,64},{128,96},{160,128},{192,160},{224,1... | collective-permute-start | bytes 3538952 | tf_op jit(solution)/shard_map/ppermute | solution.py:9
  80.4 51.0 %collective-permute-start.4 = (bf16[512,1152]{0,1:T(8,128)(2,1)S(1)}, bf16[512,1152]{0,1:T(8,128)(2,1)S(1)}, u32[]{:S(2)}, u32[]{:S(2)}) collective-permute-start(bf16[512,1152]{0,1:T(8,128)(2,1)S(1)} %get-tuple-element.8), channel_id=1, source_target_pairs={{0,1},{1,2},{2,3},{3,4},{4,5},{5,6},{6,7},{7,8},{8,9},{9,10},{10,1... | collective-permute-start | bytes 3538952 | tf_op jit(solution)/shard_map/ppermute | solution.py:9
where the time goes:
time: 137 us; the launch traced here: 135 us
  waiting for transfers between devices  74.3 us (54%)
  starting transfers between devices  37 us (27%)
  matrix products  13.3 us (10%)
  other arithmetic  4.72 us (3%)
  local copies, waits for them, and re-layouts  3.32 us (2%)
  between operations  2.1 us (2%)
    ppermute x6, waiting for transfers between devices, shifted(): lax.ppermute(array, axis, [(i, (i + by) % size) for i in range(size)])  74.3 us
    ppermute x6, starting transfers between devices, shifted(): lax.ppermute(array, axis, [(i, (i + by) % size) for i in range(size)])  37 us
    dot_general x1, matrix products, on_device(): image_sum = jnp.dot(weights, visiting, preferred_element_type=jnp.float32)  6.11 us
    dot_general x1, matrix products, on_device(): lax.dot_general(image_low, visiting, (((1,), (1,)), ((), ())), preferred_...  4.26 us
    unnamed x8, local copies, waits for them, and re-layouts  2.99 us
    dot_general x1, matrix products, on_device(): lax.dot_general(weights, image_low, (((0,), (0,)), ((), ())), preferred_e...  2.88 us
  transfers between devices with their start and end apart: 6, of which 3 were waited for; matrix products, arithmetic and copies ran while one was open for 6% of the time, Pallas kernels for 0%

commit v1 on v0

v1 whole, which is shorter than its diff:
```python
import jax
import jax.numpy as jnp
from jax import lax
from jax.experimental import pallas as pl
from jax.experimental.pallas import tpu as pltpu
from jax.sharding import PartitionSpec as P

AXES = ("grp", "blk")
N_GRP = 16
N_BLK = 32
PLANES = 8
TILE = 256
VMEM = pl.BlockSpec(memory_space=pltpu.VMEM)
SMEM = pl.BlockSpec(memory_space=pltpu.SMEM)


def pairs(target):
    found = []
    for group in range(N_GRP):
        for block in range(N_BLK):
            to = target(group, block)
            if to is not None:
                found.append((group * N_BLK + block, (to[0] % N_GRP) * N_BLK + to[1] % N_BLK))
    return found


def send(array, target):
    return lax.ppermute(array, AXES, pairs(target))


def chip_mate(group, block):
    return (group, block ^ 1)


def across(group, block):
    return (group, block + 1 if block % 2 else block - 1)


def unit_rows(values):
    widened = values.astype(jnp.float32)
    inverse = lax.rsqrt(jnp.sum(widened * widened, axis=1, keepdims=True) + 1e-06)
    return (widened * inverse, inverse)


def normalize_into(low_ref, raw):
    low_ref[...] = unit_rows(raw)[0].astype(jnp.bfloat16)


def scale_of(scale_ref):
    return jnp.exp(jnp.full((1, 1), scale_ref[0], jnp.float32))


def weights_of(logits, scale):
    return scale * jax.nn.sigmoid(logits)


def logits_of(left, right, scale, bias):
    scores = lax.dot_general(left, right, (((1,), (1,)), ((), ())), preferred_element_type=jnp.float32)
    return scale * scores + bias


def softplus(logits):
    return jnp.maximum(logits, 0.0) + jnp.log1p(jnp.exp(-jnp.abs(logits)))


def lane_groups(values):
    total = values[:, :128]
    for start in range(128, values.shape[1], 128):
        total = total + values[:, start : start + 128]
    return total


def tangent(raw, summed):
    units, inverse = unit_rows(raw)
    inner = jnp.sum(units * summed, axis=1, keepdims=True)
    return (inverse * (summed - units * inner)).astype(jnp.bfloat16)


def diagonal(start, shape):
    rows = lax.broadcasted_iota(jnp.int32, shape, 0) + start
    return rows == lax.broadcasted_iota(jnp.int32, shape, 1)


def dot(left, right):
    return jnp.dot(left, right, preferred_element_type=jnp.float32)


def own_kernel(
    scale_ref, bias_ref, image_ref, text_ref, image_in_ref, text_in_ref,
    image_low_ref, text_low_ref, image_sum_ref, text_sum_ref, loss_ref, image_in_low, text_in_low,
):
    scale = scale_of(scale_ref)
    bias = bias_ref[0]
    normalize_into(image_low_ref, image_ref[...])
    normalize_into(text_low_ref, text_ref[...])
    normalize_into(image_in_low, image_in_ref[...])
    normalize_into(text_in_low, text_in_ref[...])

    @pl.loop(0, image_ref.shape[0] // TILE)
    def _(step):
        start = pl.multiple_of(step * TILE, TILE)
        here = pl.ds(start, TILE)
        image_low = image_low_ref[here, :]
        text_low = text_low_ref[here, :]
        logits = logits_of(image_low, text_low_ref[...], scale, bias)
        paired = diagonal(start, logits.shape)
        loss = lane_groups(softplus(jnp.where(paired, -logits, logits)))
        weights = (weights_of(logits, scale) - jnp.where(paired, scale, 0.0)).astype(jnp.bfloat16)
        image_sum = dot(weights, text_low_ref[...])
        logits = logits_of(image_low, text_in_low[...], scale, bias)
        loss_ref[here, :] = loss + lane_groups(softplus(logits))
        weights = weights_of(logits, scale).astype(jnp.bfloat16)
        image_sum_ref[here, :] = image_sum + dot(weights, text_in_low[...])
        logits = logits_of(text_low, image_low_ref[...], scale, bias)
        paired = diagonal(start, logits.shape)
        weights = (weights_of(logits, scale) - jnp.where(paired, scale, 0.0)).astype(jnp.bfloat16)
        text_sum = dot(weights, image_low_ref[...])
        logits = logits_of(text_low, image_in_low[...], scale, bias)
        weights = weights_of(logits, scale).astype(jnp.bfloat16)
        text_sum_ref[here, :] = text_sum + dot(weights, image_in_low[...])


def text_kernel(
    scale_ref, bias_ref, text_y_ref, image_low_ref, image_sum_in, loss_in, image_sum_ref, loss_ref, low,
):
    scale = scale_of(scale_ref)
    bias = bias_ref[0]
    normalize_into(low, text_y_ref[...])

    @pl.loop(0, image_low_ref.shape[0] // TILE)
    def _(step):
        here = pl.ds(pl.multiple_of(step * TILE, TILE), TILE)
        logits = logits_of(image_low_ref[here, :], low[...], scale, bias)
        loss_ref[here, :] = loss_in[here, :] + lane_groups(softplus(logits))
        weights = weights_of(logits, scale).astype(jnp.bfloat16)
        image_sum_ref[here, :] = image_sum_in[here, :] + dot(weights, low[...])


def group_kernel(
    scale_ref, bias_ref, text_z_ref, image_z_ref, image_ref, image_low_ref, text_low_ref, image_sum_ref, text_sum_in,
    loss_in, image_grad_ref, text_sum_ref, loss_ref, image_z_low, text_z_low,
):
    scale = scale_of(scale_ref)
    bias = bias_ref[0]
    normalize_into(text_z_low, text_z_ref[...])
    normalize_into(image_z_low, image_z_ref[...])
    columns = 4 * image_ref.shape[0]

    @pl.loop(0, image_ref.shape[0] // TILE)
    def _(step):
        here = pl.ds(pl.multiple_of(step * TILE, TILE), TILE)
        logits = logits_of(image_low_ref[here, :], text_z_low[...], scale, bias)
        loss = loss_in[here, :] + lane_groups(softplus(logits))
        loss_ref[here, :] = jnp.sum(loss, axis=1, keepdims=True) * (1.0 / columns)
        weights = weights_of(logits, scale).astype(jnp.bfloat16)
        image_sum = image_sum_ref[here, :] + dot(weights, text_z_low[...])
        image_grad_ref[here, :] = tangent(image_ref[here, :], image_sum)
        logits = logits_of(text_low_ref[here, :], image_z_low[...], scale, bias)
        weights = weights_of(logits, scale).astype(jnp.bfloat16)
        text_sum_ref[here, :] = text_sum_in[here, :] + dot(weights, image_z_low[...])


def last_kernel(scale_ref, bias_ref, image_y_ref, text_ref, text_low_ref, text_sum_ref, text_grad_ref, low):
    scale = scale_of(scale_ref)
    bias = bias_ref[0]
    normalize_into(low, image_y_ref[...])

    @pl.loop(0, text_ref.shape[0] // TILE)
    def _(step):
        here = pl.ds(pl.multiple_of(step * TILE, TILE), TILE)
        logits = logits_of(text_low_ref[here, :], low[...], scale, bias)
        weights = weights_of(logits, scale).astype(jnp.bfloat16)
        text_sum = text_sum_ref[here, :] + dot(weights, low[...])
        text_grad_ref[here, :] = tangent(text_ref[here, :], text_sum)


def call(kernel, outs, scratch, scalars, arrays):
    return pl.pallas_call(
        kernel,
        out_shape=outs,
        in_specs=[SMEM] * len(scalars) + [VMEM] * len(arrays),
        out_specs=tuple(VMEM for _ in outs),
        scratch_shapes=scratch,
        compiler_params=pltpu.CompilerParams(vmem_limit_bytes=40 * 1024 * 1024),
        cost_estimate=pl.CostEstimate(flops=1000, bytes_accessed=1000, transcendentals=0),
    )(*scalars, *arrays)


def on_device(image_embed, text_embed, log_scale, bias):
    rows, width = image_embed.shape
    low = jax.ShapeDtypeStruct((rows, width), jnp.bfloat16)
    wide = jax.ShapeDtypeStruct((rows, width), jnp.float32)
    lanes = jax.ShapeDtypeStruct((rows, 128), jnp.float32)
    held = pltpu.VMEM((rows, width), jnp.bfloat16)
    scalars = (log_scale, bias)

    text_y = send(text_embed, across)
    image_y = send(image_embed, across)
    text_z = send(text_embed, lambda group, block: (group + 1, block))
    image_z = send(image_embed, lambda group, block: (group - 1, block))
    text_in = send(text_embed, chip_mate)
    image_in = send(image_embed, chip_mate)

    image_low, text_low, image_sum, text_sum, loss = call(
        own_kernel, (low, low, wide, wide, lanes), [held, held], scalars,
        (image_embed, text_embed, image_in, text_in),
    )
    image_sum, loss = call(
        text_kernel, (wide, lanes), [held], scalars, (text_y, image_low, image_sum, loss)
    )
    image_grad, text_sum, loss = call(
        group_kernel, (low, wide, jax.ShapeDtypeStruct((rows, 1), jnp.float32)), [held, held], scalars,
        (text_z, image_z, image_embed, image_low, text_low, image_sum, text_sum, loss),
    )
    (text_grad,) = call(
        last_kernel, (low,), [held], scalars, (image_y, text_embed, text_low, text_sum)
    )
    return (image_grad, text_grad, loss.reshape(rows))


def solution(mesh):
    placed = (P(AXES, None), P(AXES, None), P(), P())
    return jax.shard_map(
        on_device,
        mesh=mesh,
        in_specs=placed,
        out_specs=(P(AXES, None), P(AXES, None), P(AXES)),
        check_vma=False,
    )
```

time: 137 us -> 98.7 us (0.72)
  the two profiles are of different devices: /device:TPU:1 before, /device:TPU:6 now
where the time goes in v1:
time: 98.7 us; the launch traced here: 98.3 us
  waiting for transfers between devices  41.2 us (42%)
  starting transfers between devices  26.5 us (27%)
  Pallas kernels  22.2 us (22%)
  local copies, waits for them, and re-layouts  5.63 us (6%)
  between operations  2.02 us (2%)
    ppermute x6, waiting for transfers between devices, send(): return lax.ppermute(array, AXES, pairs(target))  41.2 us
    ppermute x6, starting transfers between devices, send(): return lax.ppermute(array, AXES, pairs(target))  26.5 us
    pallas_call x4, Pallas kernels, call(): pl.pallas_call(kernel, out_shape=outs, in_specs=[SMEM] * len(scalars) + [...  22.2 us
    unnamed x12, local copies, waits for them, and re-layouts  5.63 us
  transfers between devices with their start and end apart: 6, of which 2 were waited for; matrix products, arithmetic and copies ran while one was open for 1% of the time, Pallas kernels for 17%

profile of v1, /device:TPU:6, one launch (start us, length us, event | category | flops | bytes accessed | tf_op | source)
XLA Modules:
  0.0 98.3 jit_solution(5682374208483324428)
XLA Ops:
  0.6 1.9 %collective-permute-start.2 = (bf16[512,1152]{1,0:T(8,128)(2,1)}, bf16[512,1152]{1,0:T(8,128)(2,1)S(1)}, u32[]{:S(2)}, u32[]{:S(2)}) collective-permute-start(bf16[512,1152]{1,0:T(8,128)(2,1)} %image_ref.3), channel_id=1, source_target_pairs={{0,1},{1,0},{2,3},{3,2},{4,5},{5,4},{6,7},{7,6},{8,9},{9,8},{10,11... | collective-permute-start | bytes 3538952 | tf_op jit(solution)/shard_map/ppermute | solution.py:28
  2.6 2.4 %collective-permute-start.3 = (bf16[512,1152]{1,0:T(8,128)(2,1)}, bf16[512,1152]{1,0:T(8,128)(2,1)S(1)}, u32[]{:S(2)}, u32[]{:S(2)}) collective-permute-start(bf16[512,1152]{1,0:T(8,128)(2,1)} %text_ref.3), channel_id=1, source_target_pairs={{0,1},{1,0},{2,3},{3,2},{4,5},{5,4},{6,7},{7,6},{8,9},{9,8},{10,11... | collective-permute-start | bytes 3538952 | tf_op jit(solution)/shard_map/ppermute | solution.py:28
  5.0 6.0 %collective-permute-start.4 = (bf16[512,1152]{1,0:T(8,128)(2,1)}, bf16[512,1152]{1,0:T(8,128)(2,1)S(1)}, u32[]{:S(2)}, u32[]{:S(2)}) collective-permute-start(bf16[512,1152]{1,0:T(8,128)(2,1)} %text_ref.3), channel_id=1, source_target_pairs={{0,31},{1,2},{2,1},{3,4},{4,3},{5,6},{6,5},{7,8},{8,7},{9,10},{10,... | collective-permute-start | bytes 3538952 | tf_op jit(solution)/shard_map/ppermute | solution.py:28
  11.0 4.3 %collective-permute-start = (bf16[512,1152]{1,0:T(8,128)(2,1)}, bf16[512,1152]{1,0:T(8,128)(2,1)S(1)}, u32[]{:S(2)}, u32[]{:S(2)}) collective-permute-start(bf16[512,1152]{1,0:T(8,128)(2,1)} %text_ref.3), channel_id=1, source_target_pairs={{0,32},{1,33},{2,34},{3,35},{4,36},{5,37},{6,38},{7,39},{8,40},{9,... | collective-permute-start | bytes 3538952 | tf_op jit(solution)/shard_map/ppermute | solution.py:28
  15.3 8.7 %collective-permute-start.1 = (bf16[512,1152]{1,0:T(8,128)(2,1)}, bf16[512,1152]{1,0:T(8,128)(2,1)S(1)}, u32[]{:S(2)}, u32[]{:S(2)}) collective-permute-start(bf16[512,1152]{1,0:T(8,128)(2,1)} %image_ref.3), channel_id=1, source_target_pairs={{0,480},{1,481},{2,482},{3,483},{4,484},{5,485},{6,486},{7,487},{8... | collective-permute-start | bytes 3538952 | tf_op jit(solution)/shard_map/ppermute | solution.py:28
  24.0 0.0 collective-permute-done.2.image_in_ref
  24.0 3.1 %collective-permute-start.5 = (bf16[512,1152]{1,0:T(8,128)(2,1)}, bf16[512,1152]{1,0:T(8,128)(2,1)}, u32[]{:S(2)}, u32[]{:S(2)}) collective-permute-start(bf16[512,1152]{1,0:T(8,128)(2,1)} %image_ref.3), channel_id=1, source_target_pairs={{0,31},{1,2},{2,1},{3,4},{4,3},{5,6},{6,5},{7,8},{8,7},{9,10},{10,... | collective-permute-start | bytes 3538952 | tf_op jit(solution)/shard_map/ppermute | solution.py:28
  28.5 0.0 collective-permute-done.3.text_in_ref
  28.5 0.0 copy-start
  28.5 1.3 %copy-done = bf16[512,1152]{1,0:T(8,128)(2,1)S(1)} copy-done((bf16[512,1152]{1,0:T(8,128)(2,1)S(1)}, bf16[512,1152]{1,0:T(8,128)(2,1)}, u32[]{:S(2)}) %copy-start) | copy-done | bytes 1179672
  29.8 0.0 copy-start.2
  29.8 1.3 %copy-done.2 = bf16[512,1152]{1,0:T(8,128)(2,1)S(1)} copy-done((bf16[512,1152]{1,0:T(8,128)(2,1)S(1)}, bf16[512,1152]{1,0:T(8,128)(2,1)}, u32[]{:S(2)}) %copy-start.2) | copy-done | bytes 1179672
  31.0 8.9 %shard_map.67 = (bf16[512,1152]{1,0:T(8,128)(2,1)S(1)}, bf16[512,1152]{1,0:T(8,128)(2,1)S(1)}, f32[512,1152]{1,0:T(8,128)S(1)}, f32[512,1152]{1,0:T(8,128)S(1)}, f32[512,128]{1,0:T(8,128)S(1)}) custom-call(f32[1]{0:T(128)S(6)} %copy.7.scale_ref, f32[1]{0:T(128)S(6)} %copy.8.bias_ref, bf16[512,1152]{1,0:T(8,128)(2,1)S(1)} %copy-done, ...), custom_call_target="tpu_custom_call" | custom-call | flops 1000 | bytes 1000 | tf_op jit(solution)/shard_map/pallas_call | solution.py:178
  40.0 14.0 %collective-permute-done.4.text_y_ref = bf16[512,1152]{1,0:T(8,128)(2,1)S(1)} collective-permute-done((bf16[512,1152]{1,0:T(8,128)(2,1)}, bf16[512,1152]{1,0:T(8,128)(2,1)S(1)}, u32[]{:S(2)}, u32[]{:S(2)}) %collective-permute-start.4) | collective-permute-done | bytes 1179680 | tf_op jit(solution)/shard_map/ppermute | solution.py:28
  53.9 0.0 copy-start.1
  53.9 2.8 %shard_map.68 = (f32[512,1152]{1,0:T(8,128)S(1)}, f32[512,128]{1,0:T(8,128)S(1)}) custom-call(f32[1]{0:T(128)S(6)} %copy.7.scale_ref, f32[1]{0:T(128)S(6)} %copy.8.bias_ref, bf16[512,1152]{1,0:T(8,128)(2,1)S(1)} %collective-permute-done.4.text_y_ref, bf16[512,1152]{1,0:T(8,128)(2,1)S(1)} %get-tuple-element.13.image_low_ref, ...), custom_call_target="tpu_custom_call" | custom-call | flops 1000 | bytes 1000 | tf_op jit(solution)/shard_map/pallas_call | solution.py:178
  56.8 27.2 %collective-permute-done.text_z_ref = bf16[512,1152]{1,0:T(8,128)(2,1)S(1)} collective-permute-done((bf16[512,1152]{1,0:T(8,128)(2,1)}, bf16[512,1152]{1,0:T(8,128)(2,1)S(1)}, u32[]{:S(2)}, u32[]{:S(2)}) %collective-permute-start) | collective-permute-done | bytes 1179680 | tf_op jit(solution)/shard_map/ppermute | solution.py:28
  84.0 0.0 collective-permute-done.1.image_z_ref
  84.0 0.0 copy-done.1
  84.0 0.0 copy-start.3
  84.0 5.4 %shard_map.69 = (bf16[512,1152]{1,0:T(8,128)(2,1)}, f32[512,1152]{1,0:T(8,128)S(1)}, f32[512,1]{1,0:T(8,128)S(1)}) custom-call(f32[1]{0:T(128)S(6)} %copy.7.scale_ref, f32[1]{0:T(128)S(6)} %copy.8.bias_ref, bf16[512,1152]{1,0:T(8,128)(2,1)S(1)} %collective-permute-done.text_z_ref, bf16[512,1152]{1,0:T(8,128)(2,1)S(1)} %collective-permute-done.1.image_z_ref, ...), custom_call_target="tpu_custom_call" | custom-call | flops 1000 | bytes 1000 | tf_op jit(solution)/shard_map/pallas_call | solution.py:178
  89.4 0.0 copy-start.4
  89.4 1.4 %copy-done.4 = f32[512,1152]{1,0:T(8,128)} copy-done((f32[512,1152]{1,0:T(8,128)}, f32[512,1152]{1,0:T(8,128)S(1)}, u32[]{:S(2)}) %copy-start.4) | copy-done | bytes 2359320
  90.8 0.7 reduce
  91.5 0.0 collective-permute-done.5.image_y_ref
  91.5 0.0 copy-done.3
  91.5 0.0 copy-start.5
  91.5 1.7 %copy-done.5 = f32[512,1152]{1,0:T(8,128)S(1)} copy-done((f32[512,1152]{1,0:T(8,128)S(1)}, f32[512,1152]{1,0:T(8,128)}, u32[]{:S(2)}) %copy-start.5) | copy-done | bytes 2359320
  93.2 5.1 %shard_map.70 = bf16[512,1152]{1,0:T(8,128)(2,1)} custom-call(f32[1]{0:T(128)S(6)} %copy.7.scale_ref, f32[1]{0:T(128)S(6)} %copy.8.bias_ref, bf16[512,1152]{1,0:T(8,128)(2,1)} %collective-permute-done.5.image_y_ref, bf16[512,1152]{1,0:T(8,128)(2,1)S(1)} %copy-done.3, bf16[512,1152]{1,0:T(8,128)(2,1)S(1)} %get-tuple-element.14.text_low_ref, ...), custom_call_target="tpu_custom_call" | custom-call | flops 1000 | bytes 1000 | tf_op jit(solution)/shard_map/pallas_call | solution.py:178
Async XLA Ops:
  0.6 23.4 %collective-permute-start.2 = (bf16[512,1152]{1,0:T(8,128)(2,1)}, bf16[512,1152]{1,0:T(8,128)(2,1)S(1)}, u32[]{:S(2)}, u32[]{:S(2)}) collective-permute-start(bf16[512,1152]{1,0:T(8,128)(2,1)} %image_ref.3), channel_id=1, source_target_pairs={{0,1},{1,0},{2,3},{3,2},{4,5},{5,4},{6,7},{7,6},{8,9},{9,8},{10,11... | collective-permute-start | bytes 3538952 | tf_op jit(solution)/shard_map/ppermute | solution.py:28
  2.6 25.9 %collective-permute-start.3 = (bf16[512,1152]{1,0:T(8,128)(2,1)}, bf16[512,1152]{1,0:T(8,128)(2,1)S(1)}, u32[]{:S(2)}, u32[]{:S(2)}) collective-permute-start(bf16[512,1152]{1,0:T(8,128)(2,1)} %text_ref.3), channel_id=1, source_target_pairs={{0,1},{1,0},{2,3},{3,2},{4,5},{5,4},{6,7},{7,6},{8,9},{9,8},{10,11... | collective-permute-start | bytes 3538952 | tf_op jit(solution)/shard_map/ppermute | solution.py:28
  5.0 49.0 %collective-permute-start.4 = (bf16[512,1152]{1,0:T(8,128)(2,1)}, bf16[512,1152]{1,0:T(8,128)(2,1)S(1)}, u32[]{:S(2)}, u32[]{:S(2)}) collective-permute-start(bf16[512,1152]{1,0:T(8,128)(2,1)} %text_ref.3), channel_id=1, source_target_pairs={{0,31},{1,2},{2,1},{3,4},{4,3},{5,6},{6,5},{7,8},{8,7},{9,10},{10,... | collective-permute-start | bytes 3538952 | tf_op jit(solution)/shard_map/ppermute | solution.py:28
  11.0 73.0 %collective-permute-start = (bf16[512,1152]{1,0:T(8,128)(2,1)}, bf16[512,1152]{1,0:T(8,128)(2,1)S(1)}, u32[]{:S(2)}, u32[]{:S(2)}) collective-permute-start(bf16[512,1152]{1,0:T(8,128)(2,1)} %text_ref.3), channel_id=1, source_target_pairs={{0,32},{1,33},{2,34},{3,35},{4,36},{5,37},{6,38},{7,39},{8,40},{9,... | collective-permute-start | bytes 3538952 | tf_op jit(solution)/shard_map/ppermute | solution.py:28
  15.3 68.7 %collective-permute-start.1 = (bf16[512,1152]{1,0:T(8,128)(2,1)}, bf16[512,1152]{1,0:T(8,128)(2,1)S(1)}, u32[]{:S(2)}, u32[]{:S(2)}) collective-permute-start(bf16[512,1152]{1,0:T(8,128)(2,1)} %image_ref.3), channel_id=1, source_target_pairs={{0,480},{1,481},{2,482},{3,483},{4,484},{5,485},{6,486},{7,487},{8... | collective-permute-start | bytes 3538952 | tf_op jit(solution)/shard_map/ppermute | solution.py:28
  24.0 67.5 %collective-permute-start.5 = (bf16[512,1152]{1,0:T(8,128)(2,1)}, bf16[512,1152]{1,0:T(8,128)(2,1)}, u32[]{:S(2)}, u32[]{:S(2)}) collective-permute-start(bf16[512,1152]{1,0:T(8,128)(2,1)} %image_ref.3), channel_id=1, source_target_pairs={{0,31},{1,2},{2,1},{3,4},{4,3},{5,6},{6,5},{7,8},{8,7},{9,10},{10,... | collective-permute-start | bytes 3538952 | tf_op jit(solution)/shard_map/ppermute | solution.py:28
  28.5 1.3 %copy-start = (bf16[512,1152]{1,0:T(8,128)(2,1)S(1)}, bf16[512,1152]{1,0:T(8,128)(2,1)}, u32[]{:S(2)}) copy-start(bf16[512,1152]{1,0:T(8,128)(2,1)} %image_ref.3) | copy-start | bytes 3538948
  29.8 1.3 %copy-start.2 = (bf16[512,1152]{1,0:T(8,128)(2,1)S(1)}, bf16[512,1152]{1,0:T(8,128)(2,1)}, u32[]{:S(2)}) copy-start(bf16[512,1152]{1,0:T(8,128)(2,1)} %text_ref.3) | copy-start | bytes 3538948
  53.9 30.1 %copy-start.1 = (bf16[512,1152]{1,0:T(8,128)(2,1)S(1)}, bf16[512,1152]{1,0:T(8,128)(2,1)}, u32[]{:S(2)}) copy-start(bf16[512,1152]{1,0:T(8,128)(2,1)} %image_ref.3) | copy-start | bytes 3538948
  84.0 7.5 %copy-start.3 = (bf16[512,1152]{1,0:T(8,128)(2,1)S(1)}, bf16[512,1152]{1,0:T(8,128)(2,1)}, u32[]{:S(2)}) copy-start(bf16[512,1152]{1,0:T(8,128)(2,1)} %text_ref.3) | copy-start | bytes 3538948
  89.4 1.4 %copy-start.4 = (f32[512,1152]{1,0:T(8,128)}, f32[512,1152]{1,0:T(8,128)S(1)}, u32[]{:S(2)}) copy-start(f32[512,1152]{1,0:T(8,128)S(1)} %get-tuple-element.21.text_sum_ref) | copy-start | bytes 7077892
  91.5 1.7 %copy-start.5 = (f32[512,1152]{1,0:T(8,128)S(1)}, f32[512,1152]{1,0:T(8,128)}, u32[]{:S(2)}) copy-start(f32[512,1152]{1,0:T(8,128)} %copy-done.4) | copy-start | bytes 7077892

commit v2 on v1

v2 whole, which is shorter than its diff:
```python
import jax
import jax.numpy as jnp
from jax import lax
from jax.experimental import pallas as pl
from jax.experimental.pallas import tpu as pltpu
from jax.sharding import PartitionSpec as P

AXES = ("grp", "blk")
N_GRP = 16
N_BLK = 32
PLANES = 8
TILE = 512
VMEM = pl.BlockSpec(memory_space=pltpu.VMEM)
HBM = pl.BlockSpec(memory_space=pltpu.HBM)
PIECE = 128
UPPER_PLANES = (1, 0)
LOWER_PLANES = (2, 3)
VMEM_LIMIT = 20 * 1024 * 1024
SMEM = pl.BlockSpec(memory_space=pltpu.SMEM)


def pairs(target):
    found = []
    for group in range(N_GRP):
        for block in range(N_BLK):
            to = target(group, block)
            if to is not None:
                found.append((group * N_BLK + block, (to[0] % N_GRP) * N_BLK + to[1] % N_BLK))
    return found


def send(array, target):
    return lax.ppermute(array, AXES, pairs(target))


def chip_mate(group, block):
    return (group, block ^ 1)


def across(group, block):
    return (group, block + 1 if block % 2 else block - 1)


def upward(group, block):
    return None if group % PLANES == PLANES - 1 else (group + 1, block)


def downward(group, block):
    return None if group % PLANES == 0 else (group - 1, block)


def same_way(group, block):
    return (block + group // PLANES) % 2 == 1


def to_relay(crossed, straight):
    def target(group, block):
        half, plane = divmod(group, PLANES)
        if plane not in (0, PLANES - 1):
            return None
        moved = same_way(group, block)
        place = crossed if moved else straight
        relay = place if plane else PLANES - 1 - place
        return (half * PLANES + relay, block ^ 1 if moved else block)

    return target


def from_relay(crossed, straight):
    def target(group, block):
        half, plane = divmod(group, PLANES)
        if same_way(group, block):
            return None
        for end, place in ((0, plane), (PLANES - 1, PLANES - 1 - plane)):
            if place in (crossed, straight):
                return ((1 - half) * PLANES + end, block ^ 1 if place == crossed else block)
        return None

    return target


def unit_rows(values):
    widened = values.astype(jnp.float32)
    inverse = lax.rsqrt(jnp.sum(widened * widened, axis=1, keepdims=True) + 1e-06)
    return (widened * inverse, inverse)


def scale_of(scale_ref):
    return jnp.exp(jnp.full((1, 1), scale_ref[0], jnp.float32))


def weights_of(logits, scale):
    half = 0.5 * scale
    return half * jnp.tanh(0.5 * logits) + half


def logits_of(left, right, scale, bias):
    scores = lax.dot_general(left, right, (((1,), (1,)), ((), ())), preferred_element_type=jnp.float32)
    return scale * scores + bias


def softplus(logits):
    return jnp.log(1.0 + jnp.exp(logits))


def lane_groups(values):
    total = values[:, :128]
    for start in range(128, values.shape[1], 128):
        total = total + values[:, start : start + 128]
    return total


def tangent(raw, summed):
    units, inverse = unit_rows(raw)
    inner = jnp.sum(units * summed, axis=1, keepdims=True)
    return (inverse * (summed - units * inner)).astype(jnp.bfloat16)


def diagonal(start, shape):
    rows = lax.broadcasted_iota(jnp.int32, shape, 0) + start
    return rows == lax.broadcasted_iota(jnp.int32, shape, 1)


def dot(left, right):
    return jnp.dot(left, right, preferred_element_type=jnp.float32)


def unit_kernel(image_ref, text_ref, pair_ref):
    rows = image_ref.shape[0]
    for start in range(0, rows, PIECE):
        here = pl.ds(start, PIECE)
        pair_ref[here, :] = unit_rows(image_ref[here, :])[0].astype(jnp.bfloat16)
        pair_ref[pl.ds(rows + start, PIECE), :] = unit_rows(text_ref[here, :])[0].astype(jnp.bfloat16)


def pick_kernel(pair_ref, pair_in_ref, upper_ref, lower_ref, image_out_ref, text_out_ref):
    del pair_in_ref
    low_plane = lax.axis_index("grp") % PLANES < PLANES // 2
    rows = image_out_ref.shape[0]
    half = rows // 2
    image_low, text_low = pair_ref[:rows, :], pair_ref[rows:, :]
    upper_ref[...] = jnp.where(low_plane, image_low[:half, :], text_low[:half, :])
    lower_ref[...] = jnp.where(low_plane, image_low[half:, :], text_low[half:, :])
    image_out_ref[...] = image_low
    text_out_ref[...] = text_low


def onward_kernel(relay_ref, after_ref, onward_ref):
    del after_ref
    onward_ref[...] = relay_ref[...]


def own_kernel(scale_ref, bias_ref, pair_ref, pair_in_ref, image_sum_ref, text_sum_ref, loss_ref):
    rows = image_sum_ref.shape[0]
    image_low_ref, text_low_ref = pair_ref.at[:rows, :], pair_ref.at[rows:, :]
    image_in_low, text_in_low = pair_in_ref.at[:rows, :], pair_in_ref.at[rows:, :]
    scale = scale_of(scale_ref)
    bias = bias_ref[0]

    @pl.loop(0, rows // TILE)
    def _(step):
        start = pl.multiple_of(step * TILE, TILE)
        here = pl.ds(start, TILE)
        image_low = image_low_ref[here, :]
        text_low = text_low_ref[here, :]
        logits = logits_of(image_low, text_low_ref[...], scale, bias)
        paired = diagonal(start, logits.shape)
        loss = lane_groups(softplus(jnp.where(paired, -logits, logits)))
        weights = (weights_of(logits, scale) - jnp.where(paired, scale, 0.0)).astype(jnp.bfloat16)
        image_sum = dot(weights, text_low_ref[...])
        logits = logits_of(image_low, text_in_low[...], scale, bias)
        loss_ref[here, :] = loss + lane_groups(softplus(logits))
        weights = weights_of(logits, scale).astype(jnp.bfloat16)
        image_sum_ref[here, :] = image_sum + dot(weights, text_in_low[...])
        logits = logits_of(text_low, image_low_ref[...], scale, bias)
        paired = diagonal(start, logits.shape)
        weights = (weights_of(logits, scale) - jnp.where(paired, scale, 0.0)).astype(jnp.bfloat16)
        text_sum = dot(weights, image_low_ref[...])
        logits = logits_of(text_low, image_in_low[...], scale, bias)
        weights = weights_of(logits, scale).astype(jnp.bfloat16)
        text_sum_ref[here, :] = text_sum + dot(weights, image_in_low[...])


def text_side(scale, bias, text_low, image_low_ref, image_sum_in, loss_in, image_sum_ref, loss_ref):
    logits = logits_of(image_low_ref[...], text_low, scale, bias)
    loss_ref[...] = loss_in[...] + lane_groups(softplus(logits))
    weights = weights_of(logits, scale).astype(jnp.bfloat16)
    image_sum_ref[...] = image_sum_in[...] + dot(weights, text_low)


def image_side(scale, bias, image_low, text_low_ref, text_sum_in, text_sum_ref):
    logits = logits_of(text_low_ref[...], image_low, scale, bias)
    weights = weights_of(logits, scale).astype(jnp.bfloat16)
    text_sum_ref[...] = text_sum_in[...] + dot(weights, image_low)


def mean_loss(loss, columns):
    return jnp.sum(loss.T, axis=0, keepdims=True) * (1.0 / columns)


def group_kernel(
    scale_ref, bias_ref, text_z_ref, image_z_ref, pair_ref, image_sum_in, text_sum_in, loss_in,
    image_sum_ref, text_sum_ref, loss_ref,
):
    rows = image_sum_ref.shape[0]
    image_low_ref, text_low_ref = pair_ref.at[:rows, :], pair_ref.at[rows:, :]
    scale = scale_of(scale_ref)
    bias = bias_ref[0]
    plane = lax.axis_index("grp") % PLANES

    @pl.when(plane != 0)
    def _():
        text_side(scale, bias, text_z_ref[...], image_low_ref, image_sum_in, loss_in, image_sum_ref, loss_ref)

    @pl.when(plane == 0)
    def _():
        image_sum_ref[...] = image_sum_in[...]
        loss_ref[...] = loss_in[...]

    @pl.when(plane != PLANES - 1)
    def _():
        image_side(scale, bias, image_z_ref[...], text_low_ref, text_sum_in, text_sum_ref)

    @pl.when(plane == PLANES - 1)
    def _():
        text_sum_ref[...] = text_sum_in[...]


def row_kernel(
    scale_ref, bias_ref, pair_y_ref, image_ref, text_ref, pair_ref, image_sum_in, text_sum_in,
    loss_in, image_grad_ref, text_grad_ref, image_sum_ref, text_sum_ref, loss_ref, row_loss_ref,
    image_raw, text_raw, image_grad, text_grad, reads, sems,
):
    copies = [
        pltpu.make_async_copy(image_ref, image_raw, reads.at[0]),
        pltpu.make_async_copy(text_ref, text_raw, reads.at[1]),
    ]
    for copy in copies:
        copy.start()
    scale = scale_of(scale_ref)
    bias = bias_ref[0]
    rows = image_ref.shape[0]
    plane = lax.axis_index("grp") % PLANES
    image_low_ref, text_low_ref = pair_ref.at[:rows, :], pair_ref.at[rows:, :]
    image_y_low, text_y_low = pair_y_ref[:rows, :], pair_y_ref[rows:, :]
    text_side(scale, bias, text_y_low, image_low_ref, image_sum_in, loss_in, image_sum_ref, loss_ref)
    row_loss_ref[...] = mean_loss(loss_ref[...], 4 * rows)
    writes = []
    for copy in copies:
        copy.wait()
    for start in range(0, rows, PIECE):
        here = pl.ds(start, PIECE)
        image_grad[here, :] = tangent(image_raw[here, :], image_sum_ref[here, :])
        writes.append(pltpu.make_async_copy(image_grad.at[here, :], image_grad_ref.at[here, :], sems.at[len(writes)]))
        writes[-1].start()
    image_side(scale, bias, image_y_low, text_low_ref, text_sum_in, text_sum_ref)
    for start in range(0, rows, PIECE):
        here = pl.ds(start, PIECE)
        text_grad[here, :] = tangent(text_raw[here, :], text_sum_ref[here, :])
        writes.append(pltpu.make_async_copy(text_grad.at[here, :], text_grad_ref.at[here, :], sems.at[len(writes)]))
        writes[-1].start()
    for copy in writes:
        copy.wait()


def far_kernel(
    scale_ref, bias_ref, upper_ref, lower_ref, image_ref, text_ref, pair_ref, image_sum_ref,
    text_sum_ref, loss_ref, row_loss_in, image_grad_in, text_grad_in, image_grad_ref, text_grad_ref, row_loss_ref,
    far, raw, summed, grad, read, sems,
):
    del image_grad_in, text_grad_in
    scale = scale_of(scale_ref)
    bias = bias_ref[0]
    rows = image_ref.shape[0]
    half = rows // 2
    image_low_ref, text_low_ref = pair_ref.at[:rows, :], pair_ref.at[rows:, :]
    plane = lax.axis_index("grp") % PLANES
    row_loss_ref[...] = row_loss_in[...]

    def finish(grad_ref):
        writes = []
        for start in range(0, rows, PIECE):
            here = pl.ds(start, PIECE)
            grad[here, :] = tangent(raw[here, :], summed[here, :])
            writes.append(pltpu.make_async_copy(grad.at[here, :], grad_ref.at[here, :], sems.at[len(writes)]))
            writes[-1].start()
        for copy in writes:
            copy.wait()

    @pl.when(plane == 0)
    def _():
        copy = pltpu.make_async_copy(image_ref, raw, read)
        copy.start()
        far[:half, :] = upper_ref[...]
        far[half:, :] = lower_ref[...]
        text_side(scale, bias, far[...], image_low_ref, image_sum_ref, loss_ref, summed, loss_ref)
        row_loss_ref[...] = mean_loss(loss_ref[...], 4 * rows)
        copy.wait()
        finish(image_grad_ref)

    @pl.when(plane == PLANES - 1)
    def _():
        copy = pltpu.make_async_copy(text_ref, raw, read)
        copy.start()
        far[:half, :] = upper_ref[...]
        far[half:, :] = lower_ref[...]
        image_side(scale, bias, far[...], text_low_ref, text_sum_ref, summed)
        copy.wait()
        finish(text_grad_ref)


def call(kernel, outs, scratch, scalars, arrays, in_hbm=(), out_hbm=(), aliases={}):
    return pl.pallas_call(
        kernel,
        out_shape=outs,
        in_specs=[SMEM] * len(scalars) + [HBM if i in in_hbm else VMEM for i in range(len(arrays))],
        out_specs=tuple(HBM if i in out_hbm else VMEM for i in range(len(outs))),
        scratch_shapes=scratch,
        input_output_aliases={len(scalars) + i: o for i, o in aliases.items()},
        compiler_params=pltpu.CompilerParams(vmem_limit_bytes=VMEM_LIMIT),
        cost_estimate=pl.CostEstimate(flops=1000, bytes_accessed=1000, transcendentals=0),
    )(*scalars, *arrays)


def some(rows, width=1152):
    return jax.ShapeDtypeStruct((rows, width), jnp.bfloat16)


def on_device(image_embed, text_embed, log_scale, bias):
    rows, width = image_embed.shape
    low = jax.ShapeDtypeStruct((rows, width), jnp.bfloat16)
    pair = jax.ShapeDtypeStruct((2 * rows, width), jnp.bfloat16)
    half = jax.ShapeDtypeStruct((rows // 2, width), jnp.bfloat16)
    wide = jax.ShapeDtypeStruct((rows, width), jnp.float32)
    lanes = jax.ShapeDtypeStruct((rows, 128), jnp.float32)
    held = pltpu.VMEM((rows, width), jnp.bfloat16)
    scalars = (log_scale, bias)

    (pair_low,) = call(unit_kernel, (pair,), [], (), (image_embed, text_embed))
    pair_in = send(pair_low, chip_mate)
    pair_y = send(pair_low, across)
    upper, lower, image_out, text_out = call(
        pick_kernel, (half, half, low, low), [], (), (pair_low, pair_in), (1,)
    )
    upper_relay = send(upper, to_relay(*UPPER_PLANES))
    lower_relay = send(lower, to_relay(*LOWER_PLANES))
    text_z = send(text_out, upward)
    image_z = send(image_out, downward)

    image_sum, text_sum, loss = call(
        own_kernel, (wide, wide, lanes), [], scalars, (pair_low, pair_in)
    )
    upper_far, lower_far = (
        send(call(onward_kernel, (half,), [], (), (relay, loss), (1,))[0], from_relay(*planes))
        for relay, planes in ((upper_relay, UPPER_PLANES), (lower_relay, LOWER_PLANES))
    )
    image_sum, text_sum, loss = call(
        group_kernel, (wide, wide, lanes), [], scalars,
        (text_z, image_z, pair_low, image_sum, text_sum, loss), aliases={3: 0, 4: 1, 5: 2},
    )
    row = jax.ShapeDtypeStruct((1, rows), jnp.float32)
    pieces = rows // PIECE
    image_grad, text_grad, image_sum, text_sum, loss, row_loss = call(
        row_kernel, (low, low, wide, wide, lanes, row),
        [held, held, held, held, pltpu.SemaphoreType.DMA((2,)), pltpu.SemaphoreType.DMA((2 * pieces,))], scalars,
        (pair_y, image_embed, text_embed, pair_low, image_sum, text_sum, loss),
        (1, 2), (0, 1), {4: 2, 5: 3, 6: 4},
    )
    image_grad, text_grad, loss = call(
        far_kernel, (low, low, row),
        [held, held, pltpu.VMEM((rows, width), jnp.float32), held, pltpu.SemaphoreType.DMA,
         pltpu.SemaphoreType.DMA((pieces,))], scalars,
        (upper_far, lower_far, image_embed, text_embed, pair_low, image_sum, text_sum, loss, row_loss,
         image_grad, text_grad),
        (2, 3, 9, 10), (0, 1), {9: 0, 10: 1},
    )
    return (image_grad, text_grad, loss.reshape(rows))


def solution(mesh):
    placed = (P(AXES, None), P(AXES, None), P(), P())
    return jax.shard_map(
        on_device,
        mesh=mesh,
        in_specs=placed,
        out_specs=(P(AXES, None), P(AXES, None), P(AXES)),
        check_vma=False,
    )
```

time: 98.7 us -> 91.6 us (0.928)
  the two profiles are of different devices: /device:TPU:6 before, /device:TPU:1 now
where the time goes in v2:
time: 91.6 us; the launch traced here: 91.2 us
  waiting for transfers between devices  35.2 us (38%)
  starting transfers between devices  30 us (33%)
  Pallas kernels  21.3 us (23%)
  local copies, waits for them, and re-layouts  2.54 us (3%)
  between operations  2.2 us (2%)
    ppermute x8, waiting for transfers between devices, send(): return lax.ppermute(array, AXES, pairs(target))  35.2 us
    ppermute x8, starting transfers between devices, send(): return lax.ppermute(array, AXES, pairs(target))  30 us
    pallas_call x8, Pallas kernels, call(): pl.pallas_call(kernel, out_shape=outs, in_specs=[SMEM] * len(scalars) + [...  21.3 us
    unnamed x8, local copies, waits for them, and re-layouts  2.54 us
  transfers between devices with their start and end apart: 8, of which 6 were waited for; matrix products, arithmetic and copies ran while one was open for 0% of the time, Pallas kernels for 18%

profile of v2, /device:TPU:1, one launch (start us, length us, event | category | flops | bytes accessed | tf_op | source)
XLA Modules:
  0.0 91.2 jit_solution(1547702609393008370)
XLA Ops:
  0.6 0.0 copy-start
  0.6 1.3 %copy-done = bf16[512,1152]{1,0:T(8,128)(2,1)S(1)} copy-done((bf16[512,1152]{1,0:T(8,128)(2,1)S(1)}, bf16[512,1152]{1,0:T(8,128)(2,1)}, u32[]{:S(2)}) %copy-start) | copy-done | bytes 1179672
  1.9 0.0 copy-start.2
  1.9 1.3 %copy-done.2 = bf16[512,1152]{1,0:T(8,128)(2,1)S(1)} copy-done((bf16[512,1152]{1,0:T(8,128)(2,1)S(1)}, bf16[512,1152]{1,0:T(8,128)(2,1)}, u32[]{:S(2)}) %copy-start.2) | copy-done | bytes 1179672
  3.2 0.7 shard_map.67.pair_ref
  3.9 8.8 %collective-permute-start = (bf16[1024,1152]{1,0:T(8,128)(2,1)S(1)}, bf16[1024,1152]{1,0:T(8,128)(2,1)S(1)}, u32[]{:S(2)}, u32[]{:S(2)}) collective-permute-start(bf16[1024,1152]{1,0:T(8,128)(2,1)S(1)} %shard_map.67.pair_ref), channel_id=1, source_target_pairs={{0,1},{1,0},{2,3},{3,2},{4,5},{5,4},{6,7},{7,6},{8,9},{9,8},{10,11... | collective-permute-start | bytes 7077896 | tf_op jit(solution)/shard_map/ppermute | solution.py:33
  12.7 1.9 %collective-permute-start.5 = (bf16[1024,1152]{1,0:T(8,128)(2,1)S(1)}, bf16[1024,1152]{1,0:T(8,128)(2,1)S(1)}, u32[]{:S(2)}, u32[]{:S(2)}) collective-permute-start(bf16[1024,1152]{1,0:T(8,128)(2,1)S(1)} %shard_map.67.pair_ref), channel_id=1, source_target_pairs={{0,31},{1,2},{2,1},{3,4},{4,3},{5,6},{6,5},{7,8},{8,7},{9,10},{10,... | collective-permute-start | bytes 7077896 | tf_op jit(solution)/shard_map/ppermute | solution.py:33
  14.6 2.2 %collective-permute-done.pair_in_ref = bf16[1024,1152]{1,0:T(8,128)(2,1)S(1)} collective-permute-done((bf16[1024,1152]{1,0:T(8,128)(2,1)S(1)}, bf16[1024,1152]{1,0:T(8,128)(2,1)S(1)}, u32[]{:S(2)}, u32[]{:S(2)}) %collective-permute-start) | collective-permute-done | bytes 2359328 | tf_op jit(solution)/shard_map/ppermute | solution.py:33
  16.8 0.3 shard_map.68
  17.2 1.4 %collective-permute-start.6 = (bf16[512,1152]{1,0:T(8,128)(2,1)S(1)}, bf16[512,1152]{1,0:T(8,128)(2,1)S(1)}, u32[]{:S(2)}, u32[]{:S(2)}) collective-permute-start(bf16[512,1152]{1,0:T(8,128)(2,1)S(1)} %get-tuple-element.25), channel_id=1, source_target_pairs={{0,32},{1,33},{2,34},{3,35},{4,36},{5,37},{6,38},{7,39},{8,40},{9,... | collective-permute-start | bytes 3538952 | tf_op jit(solution)/shard_map/ppermute | solution.py:33
  18.5 1.3 %collective-permute-start.7 = (bf16[512,1152]{1,0:T(8,128)(2,1)S(1)}, bf16[512,1152]{1,0:T(8,128)(2,1)S(1)}, u32[]{:S(2)}, u32[]{:S(2)}) collective-permute-start(bf16[512,1152]{1,0:T(8,128)(2,1)S(1)} %get-tuple-element.26), channel_id=1, source_target_pairs={{32,0},{33,1},{34,2},{35,3},{36,4},{37,5},{38,6},{39,7},{40,8},{41... | collective-permute-start | bytes 3538952 | tf_op jit(solution)/shard_map/ppermute | solution.py:33
  19.8 12.7 %collective-permute-start.1 = (bf16[256,1152]{1,0:T(8,128)(2,1)S(1)}, bf16[256,1152]{1,0:T(8,128)(2,1)S(1)}, u32[]{:S(2)}, u32[]{:S(2)}) collective-permute-start(bf16[256,1152]{1,0:T(8,128)(2,1)S(1)} %get-tuple-element.22), channel_id=1, source_target_pairs={{0,224},{1,192},{2,226},{3,194},{4,228},{5,196},{6,230},{7,198},{8... | collective-permute-start | bytes 1769480 | tf_op jit(solution)/shard_map/ppermute | solution.py:33
  32.6 1.3 %collective-permute-start.3 = (bf16[256,1152]{1,0:T(8,128)(2,1)S(1)}, bf16[256,1152]{1,0:T(8,128)(2,1)S(1)}, u32[]{:S(2)}, u32[]{:S(2)}) collective-permute-start(bf16[256,1152]{1,0:T(8,128)(2,1)S(1)} %get-tuple-element.24), channel_id=1, source_target_pairs={{0,128},{1,160},{2,130},{3,162},{4,132},{5,164},{6,134},{7,166},{8... | collective-permute-start | bytes 1769480 | tf_op jit(solution)/shard_map/ppermute | solution.py:33
  35.2 6.7 %shard_map.69 = (f32[512,1152]{1,0:T(8,128)S(1)}, f32[512,1152]{1,0:T(8,128)S(1)}, f32[512,128]{1,0:T(8,128)S(1)}) custom-call(f32[1]{0:T(128)S(6)} %copy.23.scale_ref, f32[1]{0:T(128)S(6)} %copy.24.bias_ref, bf16[1024,1152]{1,0:T(8,128)(2,1)S(1)} %shard_map.67.pair_ref, bf16[1024,1152]{1,0:T(8,128)(2,1)S(1)} %collective-permute-done.pair_in_ref), custom_call_target="tpu_custom_call" | custom-call | flops 1000 | bytes 1000 | tf_op jit(solution)/shard_map/pallas_call | solution.py:313
  41.9 3.1 %collective-permute-done.1.relay_ref = bf16[256,1152]{1,0:T(8,128)(2,1)S(1)} collective-permute-done((bf16[256,1152]{1,0:T(8,128)(2,1)S(1)}, bf16[256,1152]{1,0:T(8,128)(2,1)S(1)}, u32[]{:S(2)}, u32[]{:S(2)}) %collective-permute-start.1) | collective-permute-done | bytes 589856 | tf_op jit(solution)/shard_map/ppermute | solution.py:33
  45.1 1.3 %collective-permute-start.2 = (bf16[256,1152]{1,0:T(8,128)(2,1)S(1)}, bf16[256,1152]{1,0:T(8,128)(2,1)S(1)}, u32[]{:S(2)}, u32[]{:S(2)}) collective-permute-start(bf16[256,1152]{1,0:T(8,128)(2,1)S(1)} %shard_map.70), channel_id=1, source_target_pairs={{0,256},{2,258},{4,260},{6,262},{8,264},{10,266},{12,268},{14,270}... | collective-permute-start | bytes 1769480 | tf_op jit(solution)/shard_map/ppermute | solution.py:33
  46.4 5.6 %collective-permute-done.3.relay_ref = bf16[256,1152]{1,0:T(8,128)(2,1)S(1)} collective-permute-done((bf16[256,1152]{1,0:T(8,128)(2,1)S(1)}, bf16[256,1152]{1,0:T(8,128)(2,1)S(1)}, u32[]{:S(2)}, u32[]{:S(2)}) %collective-permute-start.3) | collective-permute-done | bytes 589856 | tf_op jit(solution)/shard_map/ppermute | solution.py:33
  52.0 1.3 %collective-permute-start.4 = (bf16[256,1152]{1,0:T(8,128)(2,1)S(1)}, bf16[256,1152]{1,0:T(8,128)(2,1)S(1)}, u32[]{:S(2)}, u32[]{:S(2)}) collective-permute-start(bf16[256,1152]{1,0:T(8,128)(2,1)S(1)} %shard_map.71), channel_id=1, source_target_pairs={{64,257},{66,259},{68,261},{70,263},{72,265},{74,267},{76,269},{78... | collective-permute-start | bytes 1769480 | tf_op jit(solution)/shard_map/ppermute | solution.py:33
  53.3 1.3 %collective-permute-done.6.text_z_ref = bf16[512,1152]{1,0:T(8,128)(2,1)S(1)} collective-permute-done((bf16[512,1152]{1,0:T(8,128)(2,1)S(1)}, bf16[512,1152]{1,0:T(8,128)(2,1)S(1)}, u32[]{:S(2)}, u32[]{:S(2)}) %collective-permute-start.6) | collective-permute-done | bytes 1179680 | tf_op jit(solution)/shard_map/ppermute | solution.py:33
  54.7 0.0 collective-permute-done.7.image_z_ref
  54.7 0.0 copy-start.1
  54.7 0.0 copy-start.3
  54.7 2.3 %shard_map.72 = (f32[512,1152]{1,0:T(8,128)S(1)}, f32[512,1152]{1,0:T(8,128)S(1)}, f32[512,128]{1,0:T(8,128)S(1)}) custom-call(f32[1]{0:T(128)S(6)} %copy.23.scale_ref, f32[1]{0:T(128)S(6)} %copy.24.bias_ref, bf16[512,1152]{1,0:T(8,128)(2,1)S(1)} %collective-permute-done.6.text_z_ref, ...), custom_call_target="tpu_custom_call", output_to_operand_aliasing={{0}: (5, {}), {1}: (6, {}), {2}: (7, {})} | custom-call | flops 1000 | bytes 1000 | tf_op jit(solution)/shard_map/pallas_call | solution.py:313
  56.9 14.8 %collective-permute-done.5.pair_y_ref = bf16[1024,1152]{1,0:T(8,128)(2,1)S(1)} collective-permute-done((bf16[1024,1152]{1,0:T(8,128)(2,1)S(1)}, bf16[1024,1152]{1,0:T(8,128)(2,1)S(1)}, u32[]{:S(2)}, u32[]{:S(2)}) %collective-permute-start.5) | collective-permute-done | bytes 2359328 | tf_op jit(solution)/shard_map/ppermute | solution.py:33
  71.8 0.0 copy-done.1
  71.8 0.0 copy-done.3
  71.8 6.7 %shard_map.73 = (bf16[512,1152]{1,0:T(8,128)(2,1)}, bf16[512,1152]{1,0:T(8,128)(2,1)}, f32[512,1152]{1,0:T(8,128)S(1)}, f32[512,1152]{1,0:T(8,128)S(1)}, f32[512,128]{1,0:T(8,128)S(1)}, /*index=5*/f32[1,512]{1,0:T(1,128)S(1)}) custom-call(f32[1]{0:T(128)S(6)} %copy.23.scale_ref, ...), custom_call_target="tpu_custom_call", output_to_operand_aliasing={{2}: (6, {}), {3}: (7, {}), {4}: (8, {})} | custom-call | flops 1000 | bytes 1000 | tf_op jit(solution)/shard_map/pallas_call | solution.py:313
  78.5 0.0 collective-permute-done.2.upper_ref
  78.5 8.1 %collective-permute-done.4.lower_ref = bf16[256,1152]{1,0:T(8,128)(2,1)S(1)} collective-permute-done((bf16[256,1152]{1,0:T(8,128)(2,1)S(1)}, bf16[256,1152]{1,0:T(8,128)(2,1)S(1)}, u32[]{:S(2)}, u32[]{:S(2)}) %collective-permute-start.4) | collective-permute-done | bytes 589856 | tf_op jit(solution)/shard_map/ppermute | solution.py:33
  86.6 4.5 %shard_map.74 = (bf16[512,1152]{1,0:T(8,128)(2,1)}, bf16[512,1152]{1,0:T(8,128)(2,1)}, f32[1,512]{1,0:T(1,128)}) custom-call(f32[1]{0:T(128)S(6)} %copy.23.scale_ref, f32[1]{0:T(128)S(6)} %copy.24.bias_ref, bf16[256,1152]{1,0:T(8,128)(2,1)S(1)} %collective-permute-done.2.upper_ref, ...), custom_call_target="tpu_custom_call", output_to_operand_aliasing={{0}: (11, {}), {1}: (12, {})} | custom-call | flops 1000 | bytes 1000 | tf_op jit(solution)/shard_map/pallas_call | solution.py:313
  (2 shorter events, 0.1 us)
Async XLA Ops:
  0.6 1.3 %copy-start = (bf16[512,1152]{1,0:T(8,128)(2,1)S(1)}, bf16[512,1152]{1,0:T(8,128)(2,1)}, u32[]{:S(2)}) copy-start(bf16[512,1152]{1,0:T(8,128)(2,1)} %image_ref.5) | copy-start | bytes 3538948
  1.9 1.3 %copy-start.2 = (bf16[512,1152]{1,0:T(8,128)(2,1)S(1)}, bf16[512,1152]{1,0:T(8,128)(2,1)}, u32[]{:S(2)}) copy-start(bf16[512,1152]{1,0:T(8,128)(2,1)} %text_ref.5) | copy-start | bytes 3538948
  3.9 12.9 %collective-permute-start = (bf16[1024,1152]{1,0:T(8,128)(2,1)S(1)}, bf16[1024,1152]{1,0:T(8,128)(2,1)S(1)}, u32[]{:S(2)}, u32[]{:S(2)}) collective-permute-start(bf16[1024,1152]{1,0:T(8,128)(2,1)S(1)} %shard_map.67.pair_ref), channel_id=1, source_target_pairs={{0,1},{1,0},{2,3},{3,2},{4,5},{5,4},{6,7},{7,6},{8,9},{9,8},{10,11... | collective-permute-start | bytes 7077896 | tf_op jit(solution)/shard_map/ppermute | solution.py:33
  12.7 59.1 %collective-permute-start.5 = (bf16[1024,1152]{1,0:T(8,128)(2,1)S(1)}, bf16[1024,1152]{1,0:T(8,128)(2,1)S(1)}, u32[]{:S(2)}, u32[]{:S(2)}) collective-permute-start(bf16[1024,1152]{1,0:T(8,128)(2,1)S(1)} %shard_map.67.pair_ref), channel_id=1, source_target_pairs={{0,31},{1,2},{2,1},{3,4},{4,3},{5,6},{6,5},{7,8},{8,7},{9,10},{10,... | collective-permute-start | bytes 7077896 | tf_op jit(solution)/shard_map/ppermute | solution.py:33
  17.2 37.5 %collective-permute-start.6 = (bf16[512,1152]{1,0:T(8,128)(2,1)S(1)}, bf16[512,1152]{1,0:T(8,128)(2,1)S(1)}, u32[]{:S(2)}, u32[]{:S(2)}) collective-permute-start(bf16[512,1152]{1,0:T(8,128)(2,1)S(1)} %get-tuple-element.25), channel_id=1, source_target_pairs={{0,32},{1,33},{2,34},{3,35},{4,36},{5,37},{6,38},{7,39},{8,40},{9,... | collective-permute-start | bytes 3538952 | tf_op jit(solution)/shard_map/ppermute | solution.py:33
  18.5 36.1 %collective-permute-start.7 = (bf16[512,1152]{1,0:T(8,128)(2,1)S(1)}, bf16[512,1152]{1,0:T(8,128)(2,1)S(1)}, u32[]{:S(2)}, u32[]{:S(2)}) collective-permute-start(bf16[512,1152]{1,0:T(8,128)(2,1)S(1)} %get-tuple-element.26), channel_id=1, source_target_pairs={{32,0},{33,1},{34,2},{35,3},{36,4},{37,5},{38,6},{39,7},{40,8},{41... | collective-permute-start | bytes 3538952 | tf_op jit(solution)/shard_map/ppermute | solution.py:33
  19.8 25.2 %collective-permute-start.1 = (bf16[256,1152]{1,0:T(8,128)(2,1)S(1)}, bf16[256,1152]{1,0:T(8,128)(2,1)S(1)}, u32[]{:S(2)}, u32[]{:S(2)}) collective-permute-start(bf16[256,1152]{1,0:T(8,128)(2,1)S(1)} %get-tuple-element.22), channel_id=1, source_target_pairs={{0,224},{1,192},{2,226},{3,194},{4,228},{5,196},{6,230},{7,198},{8... | collective-permute-start | bytes 1769480 | tf_op jit(solution)/shard_map/ppermute | solution.py:33
  32.6 19.4 %collective-permute-start.3 = (bf16[256,1152]{1,0:T(8,128)(2,1)S(1)}, bf16[256,1152]{1,0:T(8,128)(2,1)S(1)}, u32[]{:S(2)}, u32[]{:S(2)}) collective-permute-start(bf16[256,1152]{1,0:T(8,128)(2,1)S(1)} %get-tuple-element.24), channel_id=1, source_target_pairs={{0,128},{1,160},{2,130},{3,162},{4,132},{5,164},{6,134},{7,166},{8... | collective-permute-start | bytes 1769480 | tf_op jit(solution)/shard_map/ppermute | solution.py:33
  45.1 33.4 %collective-permute-start.2 = (bf16[256,1152]{1,0:T(8,128)(2,1)S(1)}, bf16[256,1152]{1,0:T(8,128)(2,1)S(1)}, u32[]{:S(2)}, u32[]{:S(2)}) collective-permute-start(bf16[256,1152]{1,0:T(8,128)(2,1)S(1)} %shard_map.70), channel_id=1, source_target_pairs={{0,256},{2,258},{4,260},{6,262},{8,264},{10,266},{12,268},{14,270}... | collective-permute-start | bytes 1769480 | tf_op jit(solution)/shard_map/ppermute | solution.py:33
  52.0 34.6 %collective-permute-start.4 = (bf16[256,1152]{1,0:T(8,128)(2,1)S(1)}, bf16[256,1152]{1,0:T(8,128)(2,1)S(1)}, u32[]{:S(2)}, u32[]{:S(2)}) collective-permute-start(bf16[256,1152]{1,0:T(8,128)(2,1)S(1)} %shard_map.71), channel_id=1, source_target_pairs={{64,257},{66,259},{68,261},{70,263},{72,265},{74,267},{76,269},{78... | collective-permute-start | bytes 1769480 | tf_op jit(solution)/shard_map/ppermute | solution.py:33
  54.7 17.1 %copy-start.1 = (bf16[512,1152]{1,0:T(8,128)(2,1)S(1)}, bf16[512,1152]{1,0:T(8,128)(2,1)}, u32[]{:S(2)}) copy-start(bf16[512,1152]{1,0:T(8,128)(2,1)} %image_ref.5) | copy-start | bytes 3538948
  54.7 17.1 %copy-start.3 = (bf16[512,1152]{1,0:T(8,128)(2,1)S(1)}, bf16[512,1152]{1,0:T(8,128)(2,1)}, u32[]{:S(2)}) copy-start(bf16[512,1152]{1,0:T(8,128)(2,1)} %text_ref.5) | copy-start | bytes 3538948

commit v3 on v2

--- a/solution.py
+++ b/solution.py
@@ -125,24 +125,32 @@
     return jnp.dot(left, right, preferred_element_type=jnp.float32)
 
 
-def unit_kernel(image_ref, text_ref, pair_ref):
+def unit_kernel(image_ref, text_ref, pair_ref, upper_ref, lower_ref, raw, sems):
     rows = image_ref.shape[0]
-    for start in range(0, rows, PIECE):
-        here = pl.ds(start, PIECE)
-        pair_ref[here, :] = unit_rows(image_ref[here, :])[0].astype(jnp.bfloat16)
-        pair_ref[pl.ds(rows + start, PIECE), :] = unit_rows(text_ref[here, :])[0].astype(jnp.bfloat16)
-
-
-def pick_kernel(pair_ref, pair_in_ref, upper_ref, lower_ref, image_out_ref, text_out_ref):
-    del pair_in_ref
+    half = rows // 2
+    reads = []
+    for source, base in ((image_ref, 0), (text_ref, rows)):
+        for start in range(0, rows, PIECE):
+            reads.append(
+                pltpu.make_async_copy(
+                    source.at[pl.ds(start, PIECE), :], raw.at[pl.ds(base + start, PIECE), :], sems.at[len(reads)]
+                )
+            )
+            reads[-1].start()
+    for step, read in enumerate(reads):
+        here = pl.ds(step * PIECE, PIECE)
+        read.wait()
+        pair_ref[here, :] = unit_rows(raw[here, :])[0].astype(jnp.bfloat16)
     low_plane = lax.axis_index("grp") % PLANES < PLANES // 2
-    rows = image_out_ref.shape[0]
-    half = rows // 2
-    image_low, text_low = pair_ref[:rows, :], pair_ref[rows:, :]
-    upper_ref[...] = jnp.where(low_plane, image_low[:half, :], text_low[:half, :])
-    lower_ref[...] = jnp.where(low_plane, image_low[half:, :], text_low[half:, :])
-    image_out_ref[...] = image_low
-    text_out_ref[...] = text_low
+    upper_ref[...] = jnp.where(low_plane, pair_ref[:half, :], pair_ref[rows : rows + half, :])
+    lower_ref[...] = jnp.where(low_plane, pair_ref[half:rows, :], pair_ref[rows + half :, :])
+
+
+def parts_kernel(pair_ref, after_ref, image_ref, text_ref):
+    del after_ref
+    rows = image_ref.shape[0]
+    image_ref[...] = pair_ref[:rows, :]
+    text_ref[...] = pair_ref[rows:, :]
 
 
 def onward_kernel(relay_ref, after_ref, onward_ref):
@@ -263,16 +271,34 @@
         copy.wait()
 
 
+def upper_kernel(
+    scale_ref, bias_ref, upper_ref, pair_ref, image_sum_in, text_sum_in, loss_in, image_sum_ref, text_sum_ref, loss_ref
+):
+    scale = scale_of(scale_ref)
+    bias = bias_ref[0]
+    rows = image_sum_ref.shape[0]
+    plane = lax.axis_index("grp") % PLANES
+
+    @pl.when(plane == 0)
+    def _():
+        text_side(
+            scale, bias, upper_ref[...], pair_ref.at[:rows, :], image_sum_in, loss_in, image_sum_ref, loss_ref
+        )
+
+    @pl.when(plane == PLANES - 1)
+    def _():
+        image_side(scale, bias, upper_ref[...], pair_ref.at[rows:, :], text_sum_in, text_sum_ref)
+
+
 def far_kernel(
-    scale_ref, bias_ref, upper_ref, lower_ref, image_ref, text_ref, pair_ref, image_sum_ref,
+    scale_ref, bias_ref, lower_ref, image_ref, text_ref, pair_ref, image_sum_ref,
     text_sum_ref, loss_ref, row_loss_in, image_grad_in, text_grad_in, image_grad_ref, text_grad_ref, row_loss_ref,
-    far, raw, summed, grad, read, sems,
+    raw, summed, grad, read, sems,
 ):
     del image_grad_in, text_grad_in
     scale = scale_of(scale_ref)
     bias = bias_ref[0]
     rows = image_ref.shape[0]
-    half = rows // 2
     image_low_ref, text_low_ref = pair_ref.at[:rows, :], pair_ref.at[rows:, :]
     plane = lax.axis_index("grp") % PLANES
     row_loss_ref[...] = row_loss_in[...]
@@ -291,9 +317,7 @@
     def _():
         copy = pltpu.make_async_copy(image_ref, raw, read)
         copy.start()
-        far[:half, :] = upper_ref[...]
-        far[half:, :] = lower_ref[...]
-        text_side(scale, bias, far[...], image_low_ref, image_sum_ref, loss_ref, summed, loss_ref)
+        text_side(scale, bias, lower_ref[...], image_low_ref, image_sum_ref, loss_ref, summed, loss_ref)
         row_loss_ref[...] = mean_loss(loss_ref[...], 4 * rows)
         copy.wait()
         finish(image_grad_ref)
@@ -302,14 +326,12 @@
     def _():
         copy = pltpu.make_async_copy(text_ref, raw, read)
         copy.start()
-        far[:half, :] = upper_ref[...]
-        far[half:, :] = lower_ref[...]
-        image_side(scale, bias, far[...], text_low_ref, text_sum_ref, summed)
+        image_side(scale, bias, lower_ref[...], text_low_ref, text_sum_ref, summed)
         copy.wait()
         finish(text_grad_ref)
 
 
-def call(kernel, outs, scratch, scalars, arrays, in_hbm=(), out_hbm=(), aliases={}):
+def call(kernel, outs, scratch, scalars, arrays, in_hbm=(), out_hbm=(), aliases={}, vmem=VMEM_LIMIT, flops=1000):
     return pl.pallas_call(
         kernel,
         out_shape=outs,
@@ -317,8 +339,8 @@
         out_specs=tuple(HBM if i in out_hbm else VMEM for i in range(len(outs))),
         scratch_shapes=scratch,
         input_output_aliases={len(scalars) + i: o for i, o in aliases.items()},
-        compiler_params=pltpu.CompilerParams(vmem_limit_bytes=VMEM_LIMIT),
-        cost_estimate=pl.CostEstimate(flops=1000, bytes_accessed=1000, transcendentals=0),
+        compiler_params=pltpu.CompilerParams(vmem_limit_bytes=vmem),
+        cost_estimate=pl.CostEstimate(flops=flops, bytes_accessed=1000, transcendentals=0),
     )(*scalars, *arrays)
 
 
@@ -336,12 +358,15 @@
     held = pltpu.VMEM((rows, width), jnp.bfloat16)
     scalars = (log_scale, bias)
 
-    (pair_low,) = call(unit_kernel, (pair,), [], (), (image_embed, text_embed))
+    held_pair = pltpu.VMEM((2 * rows, width), jnp.bfloat16)
+    fixed = [pltpu.with_memory_space_constraint(array, pltpu.HBM) for array in (image_embed, text_embed)]
+    pair_low, upper, lower = call(
+        unit_kernel, (pair, half, half), [held_pair, pltpu.SemaphoreType.DMA((2 * rows // PIECE,))], (), fixed,
+        (0, 1),
+    )
     pair_in = send(pair_low, chip_mate)
     pair_y = send(pair_low, across)
-    upper, lower, image_out, text_out = call(
-        pick_kernel, (half, half, low, low), [], (), (pair_low, pair_in), (1,)
-    )
+    image_out, text_out = call(parts_kernel, (low, low), [], (), (pair_low, pair_in), (1,))
     upper_relay = send(upper, to_relay(*UPPER_PLANES))
     lower_relay = send(lower, to_relay(*LOWER_PLANES))
     text_z = send(text_out, upward)
@@ -351,7 +376,7 @@
         own_kernel, (wide, wide, lanes), [], scalars, (pair_low, pair_in)
     )
     upper_far, lower_far = (
-        send(call(onward_kernel, (half,), [], (), (relay, loss), (1,))[0], from_relay(*planes))
+        send(call(onward_kernel, (half,), [], (), (relay, loss), (1,), flops=5000000000)[0], from_relay(*planes))
         for relay, planes in ((upper_relay, UPPER_PLANES), (lower_relay, LOWER_PLANES))
     )
     image_sum, text_sum, loss = call(
@@ -366,13 +391,17 @@
         (pair_y, image_embed, text_embed, pair_low, image_sum, text_sum, loss),
         (1, 2), (0, 1), {4: 2, 5: 3, 6: 4},
     )
+    image_sum, text_sum, loss = call(
+        upper_kernel, (wide, wide, lanes), [], scalars, (upper_far, pair_low, image_sum, text_sum, loss),
+        aliases={2: 0, 3: 1, 4: 2},
+    )
     image_grad, text_grad, loss = call(
         far_kernel, (low, low, row),
-        [held, held, pltpu.VMEM((rows, width), jnp.float32), held, pltpu.SemaphoreType.DMA,
+        [held, pltpu.VMEM((rows, width), jnp.float32), held, pltpu.SemaphoreType.DMA,
          pltpu.SemaphoreType.DMA((pieces,))], scalars,
-        (upper_far, lower_far, image_embed, text_embed, pair_low, image_sum, text_sum, loss, row_loss,
+        (lower_far, image_embed, text_embed, pair_low, image_sum, text_sum, loss, row_loss,
          image_grad, text_grad),
-        (2, 3, 9, 10), (0, 1), {9: 0, 10: 1},
+        (1, 2, 8, 9), (0, 1), {8: 0, 9: 1},
     )
     return (image_grad, text_grad, loss.reshape(rows))
 

time: 91.6 us -> 88.1 us (0.962)
  Pallas kernels: 21.3 us -> 24.3 us
  waiting for transfers between devices: 35.2 us -> 32.2 us
  local copies, waits for them, and re-layouts: 2.54 us -> 0.01 us
  starting transfers between devices: 30 us -> 29 us
    pallas_call x8 -> x9, Pallas kernels: 21.3 us -> 24.3 us  [call(): pl.pallas_call(kernel, out_shape=outs, in_specs=[SMEM] * len(scalars) + [...]
    ppermute x8, waiting for transfers between devices: 35.2 us -> 32.2 us  [send(): return lax.ppermute(array, AXES, pairs(target))]
    unnamed x8 -> x4, local copies, waits for them, and re-layouts: 2.54 us -> 0.01 us
    ppermute x8, starting transfers between devices: 30 us -> 29 us  [send(): return lax.ppermute(array, AXES, pairs(target))]
  transfers between devices with their start and end apart: 8 -> 8, of which waited for: 6 -> 5; matrix products, arithmetic and copies ran while one was open for 0% -> 0% of each run, Pallas kernels for 18% -> 20%
where the time goes in v3:
time: 88.1 us; the launch traced here: 87.8 us
  waiting for transfers between devices  32.2 us (37%)
  starting transfers between devices  29 us (33%)
  Pallas kernels  24.3 us (28%)
  between operations  2.22 us (3%)
    ppermute x8, waiting for transfers between devices, send(): return lax.ppermute(array, AXES, pairs(target))  32.2 us
    ppermute x8, starting transfers between devices, send(): return lax.ppermute(array, AXES, pairs(target))  29 us
    pallas_call x9, Pallas kernels, call(): pl.pallas_call(kernel, out_shape=outs, in_specs=[SMEM] * len(scalars) + [...  24.3 us
  transfers between devices with their start and end apart: 8, of which 5 were waited for; matrix products, arithmetic and copies ran while one was open for 0% of the time, Pallas kernels for 20%

profile of v3, /device:TPU:1, one launch (start us, length us, event | category | flops | bytes accessed | tf_op | source)
XLA Modules:
  0.0 87.8 jit_solution(12791552030186475625)
XLA Ops:
  0.6 2.3 %shard_map.67 = (bf16[1024,1152]{1,0:T(8,128)(2,1)S(1)}, bf16[256,1152]{1,0:T(8,128)(2,1)S(1)}, bf16[256,1152]{1,0:T(8,128)(2,1)S(1)}) custom-call(bf16[512,1152]{1,0:T(8,128)(2,1)} %image_ref.5, bf16[512,1152]{1,0:T(8,128)(2,1)} %text_ref.5), custom_call_target="tpu_custom_call" | custom-call | flops 1000 | bytes 1000 | tf_op jit(solution)/shard_map/pallas_call | solution.py:335
  3.0 8.8 %collective-permute-start.1 = (bf16[1024,1152]{1,0:T(8,128)(2,1)S(1)}, bf16[1024,1152]{1,0:T(8,128)(2,1)S(1)}, u32[]{:S(2)}, u32[]{:S(2)}) collective-permute-start(bf16[1024,1152]{1,0:T(8,128)(2,1)S(1)} %get-tuple-element.27.pair_ref), channel_id=1, source_target_pairs={{0,1},{1,0},{2,3},{3,2},{4,5},{5,4},{6,7},{7,6},{8,9},{9,8},{10,11... | collective-permute-start | bytes 7077896 | tf_op jit(solution)/shard_map/ppermute | solution.py:33
  11.8 1.9 %collective-permute-start.5 = (bf16[1024,1152]{1,0:T(8,128)(2,1)S(1)}, bf16[1024,1152]{1,0:T(8,128)(2,1)S(1)}, u32[]{:S(2)}, u32[]{:S(2)}) collective-permute-start(bf16[1024,1152]{1,0:T(8,128)(2,1)S(1)} %get-tuple-element.27.pair_ref), channel_id=1, source_target_pairs={{0,31},{1,2},{2,1},{3,4},{4,3},{5,6},{6,5},{7,8},{8,7},{9,10},{10,... | collective-permute-start | bytes 7077896 | tf_op jit(solution)/shard_map/ppermute | solution.py:33
  13.7 11.8 %collective-permute-start.3 = (bf16[256,1152]{1,0:T(8,128)(2,1)S(1)}, bf16[256,1152]{1,0:T(8,128)(2,1)S(1)}, u32[]{:S(2)}, u32[]{:S(2)}) collective-permute-start(bf16[256,1152]{1,0:T(8,128)(2,1)S(1)} %get-tuple-element.29), channel_id=1, source_target_pairs={{0,224},{1,192},{2,226},{3,194},{4,228},{5,196},{6,230},{7,198},{8... | collective-permute-start | bytes 1769480 | tf_op jit(solution)/shard_map/ppermute | solution.py:33
  25.5 1.3 %collective-permute-start = (bf16[256,1152]{1,0:T(8,128)(2,1)S(1)}, bf16[256,1152]{1,0:T(8,128)(2,1)S(1)}, u32[]{:S(2)}, u32[]{:S(2)}) collective-permute-start(bf16[256,1152]{1,0:T(8,128)(2,1)S(1)} %get-tuple-element.26), channel_id=1, source_target_pairs={{0,128},{1,160},{2,130},{3,162},{4,132},{5,164},{6,134},{7,166},{8... | collective-permute-start | bytes 1769480 | tf_op jit(solution)/shard_map/ppermute | solution.py:33
  28.1 0.0 collective-permute-done.1.pair_in_ref.after_ref
  28.1 0.2 shard_map.71
  28.3 1.4 %collective-permute-start.6 = (bf16[512,1152]{1,0:T(8,128)(2,1)S(1)}, bf16[512,1152]{1,0:T(8,128)(2,1)S(1)}, u32[]{:S(2)}, u32[]{:S(2)}) collective-permute-start(bf16[512,1152]{1,0:T(8,128)(2,1)S(1)} %get-tuple-element.30), channel_id=1, source_target_pairs={{0,32},{1,33},{2,34},{3,35},{4,36},{5,37},{6,38},{7,39},{8,40},{9,... | collective-permute-start | bytes 3538952 | tf_op jit(solution)/shard_map/ppermute | solution.py:33
  29.6 1.3 %collective-permute-start.7 = (bf16[512,1152]{1,0:T(8,128)(2,1)S(1)}, bf16[512,1152]{1,0:T(8,128)(2,1)S(1)}, u32[]{:S(2)}, u32[]{:S(2)}) collective-permute-start(bf16[512,1152]{1,0:T(8,128)(2,1)S(1)} %get-tuple-element.31), channel_id=1, source_target_pairs={{32,0},{33,1},{34,2},{35,3},{36,4},{37,5},{38,6},{39,7},{40,8},{41... | collective-permute-start | bytes 3538952 | tf_op jit(solution)/shard_map/ppermute | solution.py:33
  30.9 6.7 %shard_map.68 = (f32[512,1152]{1,0:T(8,128)S(1)}, f32[512,1152]{1,0:T(8,128)S(1)}, f32[512,128]{1,0:T(8,128)S(1)}) custom-call(f32[1]{0:T(128)S(6)} %copy.29.scale_ref, f32[1]{0:T(128)S(6)} %copy.30.bias_ref, bf16[1024,1152]{1,0:T(8,128)(2,1)S(1)} %get-tuple-element.27.pair_ref, bf16[1024,1152]{1,0:T(8,128)(2,1)S(1)} %collective-permute-done.1.pair_in_ref.after_ref), custom_call_target="tpu_custom_call" | custom-call | flops 1000 | bytes 1000 | tf_op jit(solution)/shard_map/pallas_call | solution.py:335
  37.7 0.3 collective-permute-done.3.relay_ref
  38.1 1.3 %collective-permute-start.4 = (bf16[256,1152]{1,0:T(8,128)(2,1)S(1)}, bf16[256,1152]{1,0:T(8,128)(2,1)S(1)}, u32[]{:S(2)}, u32[]{:S(2)}) collective-permute-start(bf16[256,1152]{1,0:T(8,128)(2,1)S(1)} %shard_map.70), channel_id=1, source_target_pairs={{0,256},{2,258},{4,260},{6,262},{8,264},{10,266},{12,268},{14,270}... | collective-permute-start | bytes 1769480 | tf_op jit(solution)/shard_map/ppermute | solution.py:33
  39.4 5.5 %collective-permute-done.relay_ref = bf16[256,1152]{1,0:T(8,128)(2,1)S(1)} collective-permute-done((bf16[256,1152]{1,0:T(8,128)(2,1)S(1)}, bf16[256,1152]{1,0:T(8,128)(2,1)S(1)}, u32[]{:S(2)}, u32[]{:S(2)}) %collective-permute-start) | collective-permute-done | bytes 589856 | tf_op jit(solution)/shard_map/ppermute | solution.py:33
  44.9 1.3 %collective-permute-start.2 = (bf16[256,1152]{1,0:T(8,128)(2,1)S(1)}, bf16[256,1152]{1,0:T(8,128)(2,1)S(1)}, u32[]{:S(2)}, u32[]{:S(2)}) collective-permute-start(bf16[256,1152]{1,0:T(8,128)(2,1)S(1)} %shard_map.69), channel_id=1, source_target_pairs={{64,257},{66,259},{68,261},{70,263},{72,265},{74,267},{76,269},{78... | collective-permute-start | bytes 1769480 | tf_op jit(solution)/shard_map/ppermute | solution.py:33
  46.2 15.2 %collective-permute-done.6.text_z_ref = bf16[512,1152]{1,0:T(8,128)(2,1)S(1)} collective-permute-done((bf16[512,1152]{1,0:T(8,128)(2,1)S(1)}, bf16[512,1152]{1,0:T(8,128)(2,1)S(1)}, u32[]{:S(2)}, u32[]{:S(2)}) %collective-permute-start.6) | collective-permute-done | bytes 1179680 | tf_op jit(solution)/shard_map/ppermute | solution.py:33
  61.4 0.0 collective-permute-done.7.image_z_ref
  61.4 0.0 copy-start
  61.4 0.0 copy-start.1
  61.4 2.3 %shard_map.72 = (f32[512,1152]{1,0:T(8,128)S(1)}, f32[512,1152]{1,0:T(8,128)S(1)}, f32[512,128]{1,0:T(8,128)S(1)}) custom-call(f32[1]{0:T(128)S(6)} %copy.29.scale_ref, f32[1]{0:T(128)S(6)} %copy.30.bias_ref, bf16[512,1152]{1,0:T(8,128)(2,1)S(1)} %collective-permute-done.6.text_z_ref, ...), custom_call_target="tpu_custom_call", output_to_operand_aliasing={{0}: (5, {}), {1}: (6, {}), {2}: (7, {})} | custom-call | flops 1000 | bytes 1000 | tf_op jit(solution)/shard_map/pallas_call | solution.py:335
  63.7 7.2 %collective-permute-done.5.pair_y_ref = bf16[1024,1152]{1,0:T(8,128)(2,1)S(1)} collective-permute-done((bf16[1024,1152]{1,0:T(8,128)(2,1)S(1)}, bf16[1024,1152]{1,0:T(8,128)(2,1)S(1)}, u32[]{:S(2)}, u32[]{:S(2)}) %collective-permute-start.5) | collective-permute-done | bytes 2359328 | tf_op jit(solution)/shard_map/ppermute | solution.py:33
  70.8 0.0 copy-done
  70.8 0.0 copy-done.1
  70.8 6.8 %shard_map.73 = (bf16[512,1152]{1,0:T(8,128)(2,1)}, bf16[512,1152]{1,0:T(8,128)(2,1)}, f32[512,1152]{1,0:T(8,128)S(1)}, f32[512,1152]{1,0:T(8,128)S(1)}, f32[512,128]{1,0:T(8,128)S(1)}, /*index=5*/f32[1,512]{1,0:T(1,128)S(1)}) custom-call(f32[1]{0:T(128)S(6)} %copy.29.scale_ref, ...), custom_call_target="tpu_custom_call", output_to_operand_aliasing={{2}: (6, {}), {3}: (7, {}), {4}: (8, {})} | custom-call | flops 1000 | bytes 1000 | tf_op jit(solution)/shard_map/pallas_call | solution.py:335
  77.6 0.0 collective-permute-done.4.upper_ref
  77.6 1.8 %shard_map.74 = (f32[512,1152]{1,0:T(8,128)S(1)}, f32[512,1152]{1,0:T(8,128)S(1)}, f32[512,128]{1,0:T(8,128)S(1)}) custom-call(f32[1]{0:T(128)S(6)} %copy.29.scale_ref, f32[1]{0:T(128)S(6)} %copy.30.bias_ref, bf16[256,1152]{1,0:T(8,128)(2,1)S(1)} %collective-permute-done.4.upper_ref, ...), custom_call_target="tpu_custom_call", output_to_operand_aliasing={{0}: (4, {}), {1}: (5, {}), {2}: (6, {})} | custom-call | flops 1000 | bytes 1000 | tf_op jit(solution)/shard_map/pallas_call | solution.py:335
  79.5 4.0 %collective-permute-done.2.lower_ref = bf16[256,1152]{1,0:T(8,128)(2,1)S(1)} collective-permute-done((bf16[256,1152]{1,0:T(8,128)(2,1)S(1)}, bf16[256,1152]{1,0:T(8,128)(2,1)S(1)}, u32[]{:S(2)}, u32[]{:S(2)}) %collective-permute-start.2) | collective-permute-done | bytes 589856 | tf_op jit(solution)/shard_map/ppermute | solution.py:33
  83.5 4.1 %shard_map.75 = (bf16[512,1152]{1,0:T(8,128)(2,1)}, bf16[512,1152]{1,0:T(8,128)(2,1)}, f32[1,512]{1,0:T(1,128)}) custom-call(f32[1]{0:T(128)S(6)} %copy.29.scale_ref, f32[1]{0:T(128)S(6)} %copy.30.bias_ref, bf16[256,1152]{1,0:T(8,128)(2,1)S(1)} %collective-permute-done.2.lower_ref, ...), custom_call_target="tpu_custom_call", output_to_operand_aliasing={{0}: (10, {}), {1}: (11, {})} | custom-call | flops 1000 | bytes 1000 | tf_op jit(solution)/shard_map/pallas_call | solution.py:335
  (2 shorter events, 0.1 us)
Async XLA Ops:
  3.0 25.1 %collective-permute-start.1 = (bf16[1024,1152]{1,0:T(8,128)(2,1)S(1)}, bf16[1024,1152]{1,0:T(8,128)(2,1)S(1)}, u32[]{:S(2)}, u32[]{:S(2)}) collective-permute-start(bf16[1024,1152]{1,0:T(8,128)(2,1)S(1)} %get-tuple-element.27.pair_ref), channel_id=1, source_target_pairs={{0,1},{1,0},{2,3},{3,2},{4,5},{5,4},{6,7},{7,6},{8,9},{9,8},{10,11... | collective-permute-start | bytes 7077896 | tf_op jit(solution)/shard_map/ppermute | solution.py:33
  11.8 59.1 %collective-permute-start.5 = (bf16[1024,1152]{1,0:T(8,128)(2,1)S(1)}, bf16[1024,1152]{1,0:T(8,128)(2,1)S(1)}, u32[]{:S(2)}, u32[]{:S(2)}) collective-permute-start(bf16[1024,1152]{1,0:T(8,128)(2,1)S(1)} %get-tuple-element.27.pair_ref), channel_id=1, source_target_pairs={{0,31},{1,2},{2,1},{3,4},{4,3},{5,6},{6,5},{7,8},{8,7},{9,10},{10,... | collective-permute-start | bytes 7077896 | tf_op jit(solution)/shard_map/ppermute | solution.py:33
  13.7 24.3 %collective-permute-start.3 = (bf16[256,1152]{1,0:T(8,128)(2,1)S(1)}, bf16[256,1152]{1,0:T(8,128)(2,1)S(1)}, u32[]{:S(2)}, u32[]{:S(2)}) collective-permute-start(bf16[256,1152]{1,0:T(8,128)(2,1)S(1)} %get-tuple-element.29), channel_id=1, source_target_pairs={{0,224},{1,192},{2,226},{3,194},{4,228},{5,196},{6,230},{7,198},{8... | collective-permute-start | bytes 1769480 | tf_op jit(solution)/shard_map/ppermute | solution.py:33
  25.5 19.4 %collective-permute-start = (bf16[256,1152]{1,0:T(8,128)(2,1)S(1)}, bf16[256,1152]{1,0:T(8,128)(2,1)S(1)}, u32[]{:S(2)}, u32[]{:S(2)}) collective-permute-start(bf16[256,1152]{1,0:T(8,128)(2,1)S(1)} %get-tuple-element.26), channel_id=1, source_target_pairs={{0,128},{1,160},{2,130},{3,162},{4,132},{5,164},{6,134},{7,166},{8... | collective-permute-start | bytes 1769480 | tf_op jit(solution)/shard_map/ppermute | solution.py:33
  28.3 33.1 %collective-permute-start.6 = (bf16[512,1152]{1,0:T(8,128)(2,1)S(1)}, bf16[512,1152]{1,0:T(8,128)(2,1)S(1)}, u32[]{:S(2)}, u32[]{:S(2)}) collective-permute-start(bf16[512,1152]{1,0:T(8,128)(2,1)S(1)} %get-tuple-element.30), channel_id=1, source_target_pairs={{0,32},{1,33},{2,34},{3,35},{4,36},{5,37},{6,38},{7,39},{8,40},{9,... | collective-permute-start | bytes 3538952 | tf_op jit(solution)/shard_map/ppermute | solution.py:33
  29.6 31.7 %collective-permute-start.7 = (bf16[512,1152]{1,0:T(8,128)(2,1)S(1)}, bf16[512,1152]{1,0:T(8,128)(2,1)S(1)}, u32[]{:S(2)}, u32[]{:S(2)}) collective-permute-start(bf16[512,1152]{1,0:T(8,128)(2,1)S(1)} %get-tuple-element.31), channel_id=1, source_target_pairs={{32,0},{33,1},{34,2},{35,3},{36,4},{37,5},{38,6},{39,7},{40,8},{41... | collective-permute-start | bytes 3538952 | tf_op jit(solution)/shard_map/ppermute | solution.py:33
  38.1 39.6 %collective-permute-start.4 = (bf16[256,1152]{1,0:T(8,128)(2,1)S(1)}, bf16[256,1152]{1,0:T(8,128)(2,1)S(1)}, u32[]{:S(2)}, u32[]{:S(2)}) collective-permute-start(bf16[256,1152]{1,0:T(8,128)(2,1)S(1)} %shard_map.70), channel_id=1, source_target_pairs={{0,256},{2,258},{4,260},{6,262},{8,264},{10,266},{12,268},{14,270}... | collective-permute-start | bytes 1769480 | tf_op jit(solution)/shard_map/ppermute | solution.py:33
  44.9 38.6 %collective-permute-start.2 = (bf16[256,1152]{1,0:T(8,128)(2,1)S(1)}, bf16[256,1152]{1,0:T(8,128)(2,1)S(1)}, u32[]{:S(2)}, u32[]{:S(2)}) collective-permute-start(bf16[256,1152]{1,0:T(8,128)(2,1)S(1)} %shard_map.69), channel_id=1, source_target_pairs={{64,257},{66,259},{68,261},{70,263},{72,265},{74,267},{76,269},{78... | collective-permute-start | bytes 1769480 | tf_op jit(solution)/shard_map/ppermute | solution.py:33
  61.4 9.5 %copy-start = (bf16[512,1152]{1,0:T(8,128)(2,1)S(1)}, bf16[512,1152]{1,0:T(8,128)(2,1)}, u32[]{:S(2)}) copy-start(bf16[512,1152]{1,0:T(8,128)(2,1)} %image_ref.5) | copy-start | bytes 3538948
  61.4 9.5 %copy-start.1 = (bf16[512,1152]{1,0:T(8,128)(2,1)S(1)}, bf16[512,1152]{1,0:T(8,128)(2,1)}, u32[]{:S(2)}) copy-start(bf16[512,1152]{1,0:T(8,128)(2,1)} %text_ref.5) | copy-start | bytes 3538948

commit v4 on v3

--- a/solution.py
+++ b/solution.py
@@ -303,32 +303,43 @@
     plane = lax.axis_index("grp") % PLANES
     row_loss_ref[...] = row_loss_in[...]
 
-    def finish(grad_ref):
+    half = rows // 2
+
+    def finish(side, raw_source, grad_ref):
+        copy = pltpu.make_async_copy(raw_source, raw, read)
+        copy.start()
         writes = []
-        for start in range(0, rows, PIECE):
-            here = pl.ds(start, PIECE)
-            grad[here, :] = tangent(raw[here, :], summed[here, :])
-            writes.append(pltpu.make_async_copy(grad.at[here, :], grad_ref.at[here, :], sems.at[len(writes)]))
-            writes[-1].start()
+        for base in range(0, rows, half):
+            side(pl.ds(base, half))
+            if base == 0:
+                copy.wait()
+            for start in range(base, base + half, PIECE):
+                here = pl.ds(start, PIECE)
+                grad[here, :] = tangent(raw[here, :], summed[here, :])
+                writes.append(pltpu.make_async_copy(grad.at[here, :], grad_ref.at[here, :], sems.at[len(writes)]))
+                writes[-1].start()
+        row_loss_ref[...] = mean_loss(loss_ref[...], 4 * rows)
         for copy in writes:
             copy.wait()
 
     @pl.when(plane == 0)
     def _():
-        copy = pltpu.make_async_copy(image_ref, raw, read)
-        copy.start()
-        text_side(scale, bias, lower_ref[...], image_low_ref, image_sum_ref, loss_ref, summed, loss_ref)
-        row_loss_ref[...] = mean_loss(loss_ref[...], 4 * rows)
-        copy.wait()
-        finish(image_grad_ref)
+        def side(here):
+            text_side(
+                scale, bias, lower_ref[...], image_low_ref.at[here, :], image_sum_ref.at[here, :],
+                loss_ref.at[here, :], summed.at[here, :], loss_ref.at[here, :],
+            )
+
+        finish(side, image_ref, image_grad_ref)
 
     @pl.when(plane == PLANES - 1)
     def _():
-        copy = pltpu.make_async_copy(text_ref, raw, read)
-        copy.start()
-        image_side(scale, bias, lower_ref[...], text_low_ref, text_sum_ref, summed)
-        copy.wait()
-        finish(text_grad_ref)
+        def side(here):
+            image_side(
+                scale, bias, lower_ref[...], text_low_ref.at[here, :], text_sum_ref.at[here, :], summed.at[here, :]
+            )
+
+        finish(side, text_ref, text_grad_ref)
 
 
 def call(kernel, outs, scratch, scalars, arrays, in_hbm=(), out_hbm=(), aliases={}, vmem=VMEM_LIMIT, flops=1000):

time: 88.1 us -> 87.9 us (level)
  no operation moved by 1% of the time
where the time goes in v4:
time: 87.9 us; the launch traced here: 87.6 us
  waiting for transfers between devices  32.2 us (37%)
  starting transfers between devices  29 us (33%)
  Pallas kernels  24.2 us (28%)
  between operations  2.22 us (3%)
    ppermute x8, waiting for transfers between devices, send(): return lax.ppermute(array, AXES, pairs(target))  32.2 us
    ppermute x8, starting transfers between devices, send(): return lax.ppermute(array, AXES, pairs(target))  29 us
    pallas_call x9, Pallas kernels, call(): pl.pallas_call(kernel, out_shape=outs, in_specs=[SMEM] * len(scalars) + [...  24.2 us
  transfers between devices with their start and end apart: 8, of which 5 were waited for; matrix products, arithmetic and copies ran while one was open for 0% of the time, Pallas kernels for 20%

profile of v4, /device:TPU:1, one launch (start us, length us, event | category | flops | bytes accessed | tf_op | source)
XLA Modules:
  0.0 87.6 jit_solution(15368714532437827536)
XLA Ops:
  0.6 2.3 %shard_map.67 = (bf16[1024,1152]{1,0:T(8,128)(2,1)S(1)}, bf16[256,1152]{1,0:T(8,128)(2,1)S(1)}, bf16[256,1152]{1,0:T(8,128)(2,1)S(1)}) custom-call(bf16[512,1152]{1,0:T(8,128)(2,1)} %image_ref.5, bf16[512,1152]{1,0:T(8,128)(2,1)} %text_ref.5), custom_call_target="tpu_custom_call" | custom-call | flops 1000 | bytes 1000 | tf_op jit(solution)/shard_map/pallas_call | solution.py:346
  3.0 8.8 %collective-permute-start.1 = (bf16[1024,1152]{1,0:T(8,128)(2,1)S(1)}, bf16[1024,1152]{1,0:T(8,128)(2,1)S(1)}, u32[]{:S(2)}, u32[]{:S(2)}) collective-permute-start(bf16[1024,1152]{1,0:T(8,128)(2,1)S(1)} %get-tuple-element.27.pair_ref), channel_id=1, source_target_pairs={{0,1},{1,0},{2,3},{3,2},{4,5},{5,4},{6,7},{7,6},{8,9},{9,8},{10,11... | collective-permute-start | bytes 7077896 | tf_op jit(solution)/shard_map/ppermute | solution.py:33
  11.8 1.9 %collective-permute-start.5 = (bf16[1024,1152]{1,0:T(8,128)(2,1)S(1)}, bf16[1024,1152]{1,0:T(8,128)(2,1)S(1)}, u32[]{:S(2)}, u32[]{:S(2)}) collective-permute-start(bf16[1024,1152]{1,0:T(8,128)(2,1)S(1)} %get-tuple-element.27.pair_ref), channel_id=1, source_target_pairs={{0,31},{1,2},{2,1},{3,4},{4,3},{5,6},{6,5},{7,8},{8,7},{9,10},{10,... | collective-permute-start | bytes 7077896 | tf_op jit(solution)/shard_map/ppermute | solution.py:33
  13.7 11.8 %collective-permute-start.3 = (bf16[256,1152]{1,0:T(8,128)(2,1)S(1)}, bf16[256,1152]{1,0:T(8,128)(2,1)S(1)}, u32[]{:S(2)}, u32[]{:S(2)}) collective-permute-start(bf16[256,1152]{1,0:T(8,128)(2,1)S(1)} %get-tuple-element.29), channel_id=1, source_target_pairs={{0,224},{1,192},{2,226},{3,194},{4,228},{5,196},{6,230},{7,198},{8... | collective-permute-start | bytes 1769480 | tf_op jit(solution)/shard_map/ppermute | solution.py:33
  25.5 1.3 %collective-permute-start = (bf16[256,1152]{1,0:T(8,128)(2,1)S(1)}, bf16[256,1152]{1,0:T(8,128)(2,1)S(1)}, u32[]{:S(2)}, u32[]{:S(2)}) collective-permute-start(bf16[256,1152]{1,0:T(8,128)(2,1)S(1)} %get-tuple-element.26), channel_id=1, source_target_pairs={{0,128},{1,160},{2,130},{3,162},{4,132},{5,164},{6,134},{7,166},{8... | collective-permute-start | bytes 1769480 | tf_op jit(solution)/shard_map/ppermute | solution.py:33
  28.1 0.0 collective-permute-done.1.pair_in_ref.after_ref
  28.1 0.2 shard_map.71
  28.3 1.4 %collective-permute-start.6 = (bf16[512,1152]{1,0:T(8,128)(2,1)S(1)}, bf16[512,1152]{1,0:T(8,128)(2,1)S(1)}, u32[]{:S(2)}, u32[]{:S(2)}) collective-permute-start(bf16[512,1152]{1,0:T(8,128)(2,1)S(1)} %get-tuple-element.30), channel_id=1, source_target_pairs={{0,32},{1,33},{2,34},{3,35},{4,36},{5,37},{6,38},{7,39},{8,40},{9,... | collective-permute-start | bytes 3538952 | tf_op jit(solution)/shard_map/ppermute | solution.py:33
  29.6 1.3 %collective-permute-start.7 = (bf16[512,1152]{1,0:T(8,128)(2,1)S(1)}, bf16[512,1152]{1,0:T(8,128)(2,1)S(1)}, u32[]{:S(2)}, u32[]{:S(2)}) collective-permute-start(bf16[512,1152]{1,0:T(8,128)(2,1)S(1)} %get-tuple-element.31), channel_id=1, source_target_pairs={{32,0},{33,1},{34,2},{35,3},{36,4},{37,5},{38,6},{39,7},{40,8},{41... | collective-permute-start | bytes 3538952 | tf_op jit(solution)/shard_map/ppermute | solution.py:33
  30.9 6.7 %shard_map.68 = (f32[512,1152]{1,0:T(8,128)S(1)}, f32[512,1152]{1,0:T(8,128)S(1)}, f32[512,128]{1,0:T(8,128)S(1)}) custom-call(f32[1]{0:T(128)S(6)} %copy.29.scale_ref, f32[1]{0:T(128)S(6)} %copy.30.bias_ref, bf16[1024,1152]{1,0:T(8,128)(2,1)S(1)} %get-tuple-element.27.pair_ref, bf16[1024,1152]{1,0:T(8,128)(2,1)S(1)} %collective-permute-done.1.pair_in_ref.after_ref), custom_call_target="tpu_custom_call" | custom-call | flops 1000 | bytes 1000 | tf_op jit(solution)/shard_map/pallas_call | solution.py:346
  37.7 0.3 collective-permute-done.3.relay_ref
  38.1 1.3 %collective-permute-start.4 = (bf16[256,1152]{1,0:T(8,128)(2,1)S(1)}, bf16[256,1152]{1,0:T(8,128)(2,1)S(1)}, u32[]{:S(2)}, u32[]{:S(2)}) collective-permute-start(bf16[256,1152]{1,0:T(8,128)(2,1)S(1)} %shard_map.70), channel_id=1, source_target_pairs={{0,256},{2,258},{4,260},{6,262},{8,264},{10,266},{12,268},{14,270}... | collective-permute-start | bytes 1769480 | tf_op jit(solution)/shard_map/ppermute | solution.py:33
  39.4 5.5 %collective-permute-done.relay_ref = bf16[256,1152]{1,0:T(8,128)(2,1)S(1)} collective-permute-done((bf16[256,1152]{1,0:T(8,128)(2,1)S(1)}, bf16[256,1152]{1,0:T(8,128)(2,1)S(1)}, u32[]{:S(2)}, u32[]{:S(2)}) %collective-permute-start) | collective-permute-done | bytes 589856 | tf_op jit(solution)/shard_map/ppermute | solution.py:33
  44.9 1.3 %collective-permute-start.2 = (bf16[256,1152]{1,0:T(8,128)(2,1)S(1)}, bf16[256,1152]{1,0:T(8,128)(2,1)S(1)}, u32[]{:S(2)}, u32[]{:S(2)}) collective-permute-start(bf16[256,1152]{1,0:T(8,128)(2,1)S(1)} %shard_map.69), channel_id=1, source_target_pairs={{64,257},{66,259},{68,261},{70,263},{72,265},{74,267},{76,269},{78... | collective-permute-start | bytes 1769480 | tf_op jit(solution)/shard_map/ppermute | solution.py:33
  46.2 15.2 %collective-permute-done.6.text_z_ref = bf16[512,1152]{1,0:T(8,128)(2,1)S(1)} collective-permute-done((bf16[512,1152]{1,0:T(8,128)(2,1)S(1)}, bf16[512,1152]{1,0:T(8,128)(2,1)S(1)}, u32[]{:S(2)}, u32[]{:S(2)}) %collective-permute-start.6) | collective-permute-done | bytes 1179680 | tf_op jit(solution)/shard_map/ppermute | solution.py:33
  61.4 0.0 collective-permute-done.7.image_z_ref
  61.4 0.0 copy-start
  61.4 0.0 copy-start.1
  61.4 2.3 %shard_map.72 = (f32[512,1152]{1,0:T(8,128)S(1)}, f32[512,1152]{1,0:T(8,128)S(1)}, f32[512,128]{1,0:T(8,128)S(1)}) custom-call(f32[1]{0:T(128)S(6)} %copy.29.scale_ref, f32[1]{0:T(128)S(6)} %copy.30.bias_ref, bf16[512,1152]{1,0:T(8,128)(2,1)S(1)} %collective-permute-done.6.text_z_ref, ...), custom_call_target="tpu_custom_call", output_to_operand_aliasing={{0}: (5, {}), {1}: (6, {}), {2}: (7, {})} | custom-call | flops 1000 | bytes 1000 | tf_op jit(solution)/shard_map/pallas_call | solution.py:346
  63.7 7.2 %collective-permute-done.5.pair_y_ref = bf16[1024,1152]{1,0:T(8,128)(2,1)S(1)} collective-permute-done((bf16[1024,1152]{1,0:T(8,128)(2,1)S(1)}, bf16[1024,1152]{1,0:T(8,128)(2,1)S(1)}, u32[]{:S(2)}, u32[]{:S(2)}) %collective-permute-start.5) | collective-permute-done | bytes 2359328 | tf_op jit(solution)/shard_map/ppermute | solution.py:33
  70.8 0.0 copy-done
  70.8 0.0 copy-done.1
  70.8 6.8 %shard_map.73 = (bf16[512,1152]{1,0:T(8,128)(2,1)}, bf16[512,1152]{1,0:T(8,128)(2,1)}, f32[512,1152]{1,0:T(8,128)S(1)}, f32[512,1152]{1,0:T(8,128)S(1)}, f32[512,128]{1,0:T(8,128)S(1)}, /*index=5*/f32[1,512]{1,0:T(1,128)S(1)}) custom-call(f32[1]{0:T(128)S(6)} %copy.29.scale_ref, ...), custom_call_target="tpu_custom_call", output_to_operand_aliasing={{2}: (6, {}), {3}: (7, {}), {4}: (8, {})} | custom-call | flops 1000 | bytes 1000 | tf_op jit(solution)/shard_map/pallas_call | solution.py:346
  77.6 0.0 collective-permute-done.4.upper_ref
  77.6 1.8 %shard_map.74 = (f32[512,1152]{1,0:T(8,128)S(1)}, f32[512,1152]{1,0:T(8,128)S(1)}, f32[512,128]{1,0:T(8,128)S(1)}) custom-call(f32[1]{0:T(128)S(6)} %copy.29.scale_ref, f32[1]{0:T(128)S(6)} %copy.30.bias_ref, bf16[256,1152]{1,0:T(8,128)(2,1)S(1)} %collective-permute-done.4.upper_ref, ...), custom_call_target="tpu_custom_call", output_to_operand_aliasing={{0}: (4, {}), {1}: (5, {}), {2}: (6, {})} | custom-call | flops 1000 | bytes 1000 | tf_op jit(solution)/shard_map/pallas_call | solution.py:346
  79.5 4.0 %collective-permute-done.2.lower_ref = bf16[256,1152]{1,0:T(8,128)(2,1)S(1)} collective-permute-done((bf16[256,1152]{1,0:T(8,128)(2,1)S(1)}, bf16[256,1152]{1,0:T(8,128)(2,1)S(1)}, u32[]{:S(2)}, u32[]{:S(2)}) %collective-permute-start.2) | collective-permute-done | bytes 589856 | tf_op jit(solution)/shard_map/ppermute | solution.py:33
  83.5 3.9 %shard_map.75 = (bf16[512,1152]{1,0:T(8,128)(2,1)}, bf16[512,1152]{1,0:T(8,128)(2,1)}, f32[1,512]{1,0:T(1,128)}) custom-call(f32[1]{0:T(128)S(6)} %copy.29.scale_ref, f32[1]{0:T(128)S(6)} %copy.30.bias_ref, bf16[256,1152]{1,0:T(8,128)(2,1)S(1)} %collective-permute-done.2.lower_ref, ...), custom_call_target="tpu_custom_call", output_to_operand_aliasing={{0}: (10, {}), {1}: (11, {})} | custom-call | flops 1000 | bytes 1000 | tf_op jit(solution)/shard_map/pallas_call | solution.py:346
  (2 shorter events, 0.1 us)
Async XLA Ops:
  3.0 25.1 %collective-permute-start.1 = (bf16[1024,1152]{1,0:T(8,128)(2,1)S(1)}, bf16[1024,1152]{1,0:T(8,128)(2,1)S(1)}, u32[]{:S(2)}, u32[]{:S(2)}) collective-permute-start(bf16[1024,1152]{1,0:T(8,128)(2,1)S(1)} %get-tuple-element.27.pair_ref), channel_id=1, source_target_pairs={{0,1},{1,0},{2,3},{3,2},{4,5},{5,4},{6,7},{7,6},{8,9},{9,8},{10,11... | collective-permute-start | bytes 7077896 | tf_op jit(solution)/shard_map/ppermute | solution.py:33
  11.8 59.1 %collective-permute-start.5 = (bf16[1024,1152]{1,0:T(8,128)(2,1)S(1)}, bf16[1024,1152]{1,0:T(8,128)(2,1)S(1)}, u32[]{:S(2)}, u32[]{:S(2)}) collective-permute-start(bf16[1024,1152]{1,0:T(8,128)(2,1)S(1)} %get-tuple-element.27.pair_ref), channel_id=1, source_target_pairs={{0,31},{1,2},{2,1},{3,4},{4,3},{5,6},{6,5},{7,8},{8,7},{9,10},{10,... | collective-permute-start | bytes 7077896 | tf_op jit(solution)/shard_map/ppermute | solution.py:33
  13.7 24.3 %collective-permute-start.3 = (bf16[256,1152]{1,0:T(8,128)(2,1)S(1)}, bf16[256,1152]{1,0:T(8,128)(2,1)S(1)}, u32[]{:S(2)}, u32[]{:S(2)}) collective-permute-start(bf16[256,1152]{1,0:T(8,128)(2,1)S(1)} %get-tuple-element.29), channel_id=1, source_target_pairs={{0,224},{1,192},{2,226},{3,194},{4,228},{5,196},{6,230},{7,198},{8... | collective-permute-start | bytes 1769480 | tf_op jit(solution)/shard_map/ppermute | solution.py:33
  25.5 19.4 %collective-permute-start = (bf16[256,1152]{1,0:T(8,128)(2,1)S(1)}, bf16[256,1152]{1,0:T(8,128)(2,1)S(1)}, u32[]{:S(2)}, u32[]{:S(2)}) collective-permute-start(bf16[256,1152]{1,0:T(8,128)(2,1)S(1)} %get-tuple-element.26), channel_id=1, source_target_pairs={{0,128},{1,160},{2,130},{3,162},{4,132},{5,164},{6,134},{7,166},{8... | collective-permute-start | bytes 1769480 | tf_op jit(solution)/shard_map/ppermute | solution.py:33
  28.3 33.1 %collective-permute-start.6 = (bf16[512,1152]{1,0:T(8,128)(2,1)S(1)}, bf16[512,1152]{1,0:T(8,128)(2,1)S(1)}, u32[]{:S(2)}, u32[]{:S(2)}) collective-permute-start(bf16[512,1152]{1,0:T(8,128)(2,1)S(1)} %get-tuple-element.30), channel_id=1, source_target_pairs={{0,32},{1,33},{2,34},{3,35},{4,36},{5,37},{6,38},{7,39},{8,40},{9,... | collective-permute-start | bytes 3538952 | tf_op jit(solution)/shard_map/ppermute | solution.py:33
  29.6 31.7 %collective-permute-start.7 = (bf16[512,1152]{1,0:T(8,128)(2,1)S(1)}, bf16[512,1152]{1,0:T(8,128)(2,1)S(1)}, u32[]{:S(2)}, u32[]{:S(2)}) collective-permute-start(bf16[512,1152]{1,0:T(8,128)(2,1)S(1)} %get-tuple-element.31), channel_id=1, source_target_pairs={{32,0},{33,1},{34,2},{35,3},{36,4},{37,5},{38,6},{39,7},{40,8},{41... | collective-permute-start | bytes 3538952 | tf_op jit(solution)/shard_map/ppermute | solution.py:33
  38.1 39.6 %collective-permute-start.4 = (bf16[256,1152]{1,0:T(8,128)(2,1)S(1)}, bf16[256,1152]{1,0:T(8,128)(2,1)S(1)}, u32[]{:S(2)}, u32[]{:S(2)}) collective-permute-start(bf16[256,1152]{1,0:T(8,128)(2,1)S(1)} %shard_map.70), channel_id=1, source_target_pairs={{0,256},{2,258},{4,260},{6,262},{8,264},{10,266},{12,268},{14,270}... | collective-permute-start | bytes 1769480 | tf_op jit(solution)/shard_map/ppermute | solution.py:33
  44.9 38.6 %collective-permute-start.2 = (bf16[256,1152]{1,0:T(8,128)(2,1)S(1)}, bf16[256,1152]{1,0:T(8,128)(2,1)S(1)}, u32[]{:S(2)}, u32[]{:S(2)}) collective-permute-start(bf16[256,1152]{1,0:T(8,128)(2,1)S(1)} %shard_map.69), channel_id=1, source_target_pairs={{64,257},{66,259},{68,261},{70,263},{72,265},{74,267},{76,269},{78... | collective-permute-start | bytes 1769480 | tf_op jit(solution)/shard_map/ppermute | solution.py:33
  61.4 9.5 %copy-start = (bf16[512,1152]{1,0:T(8,128)(2,1)S(1)}, bf16[512,1152]{1,0:T(8,128)(2,1)}, u32[]{:S(2)}) copy-start(bf16[512,1152]{1,0:T(8,128)(2,1)} %image_ref.5) | copy-start | bytes 3538948
  61.4 9.5 %copy-start.1 = (bf16[512,1152]{1,0:T(8,128)(2,1)S(1)}, bf16[512,1152]{1,0:T(8,128)(2,1)}, u32[]{:S(2)}) copy-start(bf16[512,1152]{1,0:T(8,128)(2,1)} %text_ref.5) | copy-start | bytes 3538948
